TPU v7x, 32 devices: a whole 2x2x4 slice. The times are simulated.
32 devices in a mesh: groups: 2 (over y), seq: 4 (over z), expert: 4 (over x, core), tensor: 1.
Axes of the slice: x: 2, y: 2, z: 4, core: 2. Of those that a mesh axis runs over, the one named last changes fastest.
Arguments:
- text_tokens: bfloat16 [1024, 2560], P(('groups', 'seq', 'expert'), 'tensor'), parts along dimension 0, may hold values from -6 to 6
- panels: bfloat16 [512, 8, 2560], P(('groups', 'seq', 'expert'), None, 'tensor'), parts along dimension 0, may hold values from -6 to 6
- panel_target: int32 [512], P(('groups', 'seq', 'expert')), parts along dimension 0, may hold values from 0 to 255, as said below
- expert_ids: int32 [5120, 6], P(('groups', 'seq', 'expert')), parts along dimension 0, may hold values from 0 to 15, all different within a row; in each aligned block of 160 rows (0 to 159, 160 to 319, ...) at most 120 rows name the same one
- gate_weights: float32 [5120, 6], P(('groups', 'seq', 'expert')), parts along dimension 0, may hold values from 0.05 to 0.5
- gate_up_weight: bfloat16 [16, 2, 1408, 2560], P(('seq', 'expert'), None, 'tensor'), may hold values from -0.125 to 0.125
- down_weight: bfloat16 [16, 1408, 2560], P(('seq', 'expert'), 'tensor'), may hold values from -0.15625 to 0.15625
Outputs:
- mixed_out: bfloat16 [5120, 2560], P(('groups', 'seq', 'expert'), 'tensor'), parts along dimension 0
There are 2 independent parts, one for each index of `groups`. A program takes and returns all parts, laid end to end along the dimension named above; an argument that names none is the same for every part. Nothing has to cross between parts.
Inputs may be any that keep to these rules, and one draw needn't show every extreme that they name: `panel_target`: every value appears once. A panel held by owner index d targets an owner with the same index along expert (d % 4 equal). One owner sends at most 6 of its panels to one owner, and exactly 6 to some owner. `expert_ids`: the 6 experts of a token differ. Among the 160 tokens of one owner (aligned blocks of rows), no expert is named more than 120 times.
All inputs are finite; a program needn't handle non-finite values.
Results may differ from a plain program's by a relative error of at most 0.0057.
Values may be sent and summed in bfloat16 or wider, within the bound.
No kernel may reach another device: no remote copies, remote signals or barrier semaphores. Data moves between devices by JAX's collectives and lax.ppermute only.
A program may use at most 128 MiB of HBM per device.

v0:
```python
import functools

import jax
import jax.numpy as jnp
import numpy as np
from jax import lax
from jax.experimental import pallas as pl
from jax.experimental.pallas import tpu as pltpu
from jax.sharding import PartitionSpec as P

AXES = ("seq", "expert")


def slot_shards(
    text_tokens, panels, panel_target, expert_ids, gate_weights, gate_up_weight, down_weight
):
    seq_count = lax.axis_size("seq")
    expert_count = lax.axis_size("expert")
    owner_count = seq_count * expert_count
    pan_count = panels.shape[0]
    cap_panel = max(2, (3 * pan_count + 2 * seq_count - 1) // (2 * seq_count))
    slot_range = jnp.arange(pan_count, dtype=jnp.int32)
    owner_dev = panel_target // pan_count
    dest_seq = owner_dev // expert_count
    dest_slot = panel_target % pan_count
    onehot = (dest_seq[:, None] == jnp.arange(seq_count, dtype=jnp.int32)[None, :]).astype(
        jnp.int32
    )
    earlier = jnp.cumsum(onehot, axis=0) - onehot
    placing = dest_seq * cap_panel + jnp.sum(earlier * onehot, axis=1)
    outgoing = (
        jnp.zeros((seq_count * cap_panel,) + panels.shape[1:], panels.dtype).at[placing].set(panels)
    )
    labels = jnp.full((seq_count * cap_panel,), -1, jnp.int32).at[placing].set(dest_slot)
    arrived, arrived_labels = (
        lax.all_to_all(outgoing, "seq", split_axis=0, concat_axis=0, tiled=True),
        lax.all_to_all(labels, "seq", split_axis=0, concat_axis=0, tiled=True),
    )
    matches = (arrived_labels[None, :] == slot_range[:, None]).astype(jnp.bfloat16)
    image_rows = jnp.einsum(
        "qn,nrd->qrd", matches, arrived, preferred_element_type=jnp.float32
    ).astype(jnp.bfloat16)
    half_rows = jnp.concatenate([text_tokens, image_rows.reshape(-1, image_rows.shape[-1])], axis=0)
    tokens = lax.all_gather(half_rows, "tensor", axis=1, tiled=True)
    feature_width = tokens.shape[1]
    tok_count, top_count = expert_ids.shape
    experts_all = owner_count * gate_up_weight.shape[0]
    capacity = slot_capacity(tok_count, top_count, experts_all)
    flat_ids = expert_ids.reshape(-1)
    onehot_ids = (flat_ids[:, None] == jnp.arange(experts_all, dtype=jnp.int32)[None, :]).astype(
        jnp.int32
    )
    before = jnp.cumsum(onehot_ids, axis=0) - onehot_ids
    placing_ids = flat_ids * capacity + jnp.sum(before * onehot_ids, axis=1)
    source_rows = jnp.arange(tok_count * top_count, dtype=jnp.int32) // top_count
    outgoing_rows = (
        jnp.zeros((experts_all * capacity, feature_width), tokens.dtype)
        .at[placing_ids]
        .set(tokens[source_rows])
    )
    load_counts = jnp.sum(onehot_ids, axis=0).reshape(experts_all, 1)
    outgoing_rows = outgoing_rows.reshape(experts_all, capacity, feature_width)
    pair_weight = gate_up_weight[0]
    out_weight = down_weight[0]
    arrived_rows, arrived_loads = (
        lax.all_to_all(outgoing_rows, AXES, split_axis=0, concat_axis=0, tiled=True),
        lax.all_to_all(load_counts, AXES, split_axis=0, concat_axis=0, tiled=True),
    )
    arrived_rows = arrived_rows.reshape(-1, feature_width)
    slot_total = arrived_rows.shape[0]
    slot_index = jnp.arange(capacity, dtype=jnp.int32)
    is_live = (slot_index[None, :] < arrived_loads).reshape(-1)
    live_int = is_live.astype(jnp.int32)
    compact_at = jnp.cumsum(live_int) - live_int
    live_total = jnp.sum(live_int)
    compact_src = (
        jnp.zeros((slot_total,), jnp.int32)
        .at[jnp.where(is_live, compact_at, slot_total)]
        .set(jnp.arange(slot_total, dtype=jnp.int32), mode="drop")
    )

    def expert_block(block_no, partial_out):
        chosen = lax.dynamic_slice_in_dim(compact_src, block_no * 128, 128)
        block_rows = arrived_rows[chosen]
        gate_up = jnp.einsum(
            "rd,gfd->grf", block_rows, pair_weight, preferred_element_type=jnp.float32
        )
        hidden = (jax.nn.silu(gate_up[0]) * gate_up[1]).astype(jnp.bfloat16)
        result = jnp.dot(hidden, out_weight, preferred_element_type=jnp.float32)
        return lax.dynamic_update_slice_in_dim(partial_out, result, block_no * 128, 0)

    block_total = (live_total + 127) // 128
    padded_total = (slot_total + 127) // 128 * 128
    partial_out = lax.fori_loop(
        0, block_total, expert_block, jnp.zeros((padded_total, feature_width), jnp.float32)
    )
    summed = lax.psum_scatter(partial_out, "tensor", scatter_dimension=1, tiled=True).astype(
        jnp.bfloat16
    )
    out_width = summed.shape[1]
    returned = jnp.where(
        is_live[:, None], summed[jnp.where(is_live, compact_at, 0)], jnp.zeros((), jnp.bfloat16)
    )
    came_back = lax.all_to_all(
        returned.reshape(experts_all, capacity, out_width),
        AXES,
        split_axis=0,
        concat_axis=0,
        tiled=True,
    )
    half_width = came_back.shape[2]
    picked = came_back.reshape(-1, half_width)[placing_ids].reshape(
        tok_count, top_count, half_width
    )
    mixed_out = jnp.sum(gate_weights[:, :, None] * picked.astype(jnp.float32), axis=1)
    return mixed_out.astype(jnp.bfloat16)


def slot_capacity(tok_count, top_count, experts_all):
    return min(tok_count, (2 * tok_count * top_count // experts_all + 7) // 8 * 8)


class Ring:
    def __init__(self, seq_count, expert_count):
        self.seq, self.expert = seq_count, expert_count
        self.chips = 2 * seq_count
        self.half = seq_count
        self.devices = seq_count * expert_count
        self.slot_count = 4 * self.half
        self.owner_of = np.zeros((self.devices, self.slot_count), np.int32)
        self.sources_of = np.zeros((self.devices, self.slot_count, seq_count), np.int32)
        for d in range(self.devices):
            p, c = self.place(d)
            slots = [(0, 0), (0, 1), (self.half, 0), (self.half, 1)]
            for s in range(1, self.half):
                along = -s if c else s
                slots += [(-along, 0), (-along, 1), (along, 0), (along, 1)]
            slot_of = {(r % self.chips, k): i for i, (r, k) in enumerate(slots)}
            for i, (r, k) in enumerate(slots):
                q = (p + r) % self.chips
                self.owner_of[d, i] = self.device(q, c ^ k)
                x = q // seq_count
                for z in range(seq_count):
                    pos = z if x == 0 else self.chips - 1 - z
                    self.sources_of[d, i, z] = slot_of[((pos - p) % self.chips, k)]

    def place(self, d):
        z, e = divmod(d, self.expert)
        x, c = divmod(e, 2)
        return (z if x == 0 else self.chips - 1 - z), c

    def device(self, pos, c):
        x, z = (0, pos) if pos < self.seq else (1, self.chips - 1 - pos)
        return z * self.expert + x * 2 + c

    def step(self):
        pairs = []
        for d in range(self.devices):
            p, c = self.place(d)
            pairs.append((d, self.device((p + (-1 if c else 1)) % self.chips, c)))
        return pairs

    def swap(self):
        return [(d, d ^ 1) for d in range(self.devices)]


def kept(array):
    return pltpu.with_memory_space_constraint(array, pltpu.VMEM)


def distant(array):
    return pltpu.with_memory_space_constraint(array, pltpu.HBM)


def steps(count, unroll, body):
    if unroll:
        for i in range(count):
            body(i)
    else:
        pl.loop(0, count)(body)


def chunk_start(i, chunk):
    return i * chunk if isinstance(i, int) else pl.multiple_of(i * chunk, chunk)


def pack_kernel(
    experts, expert_count, text_ref, panels_ref, target_hbm, ids_hbm, gates_hbm, out_ref,
    target_ref, ids_ref, gates_ref, sems,
):
    text_rows, wide = text_ref.shape
    rows, width = out_ref.shape[0], out_ref.shape[1] - wide
    pan_count = target_ref.shape[1]
    panel_rows = (rows - text_rows) // pan_count
    copies = [
        pltpu.make_async_copy(text_ref, out_ref.at[:text_rows, :wide], sems.at[0]),
        pltpu.make_async_copy(panels_ref, out_ref.at[text_rows:, :wide], sems.at[1]),
    ]
    tables = [
        pltpu.make_async_copy(target_hbm, target_ref, sems.at[2]),
        pltpu.make_async_copy(ids_hbm, ids_ref, sems.at[3]),
        pltpu.make_async_copy(gates_hbm, gates_ref, sems.at[4]),
    ]
    for copy in tables + copies:
        copy.start()
    for copy in tables:
        copy.wait()
    lane = lax.broadcasted_iota(jnp.int32, (rows, width), 1)
    term = sum((lane >= i * experts).astype(jnp.int32) for i in range(1, 4))
    expert = (lane - term * experts).astype(jnp.float32)
    diagonal = lax.broadcasted_iota(jnp.int32, (rows, rows), 0) == lax.broadcasted_iota(
        jnp.int32, (rows, rows), 1
    )

    def upright(row):
        return jnp.sum(jnp.where(diagonal, row, 0.0), axis=1, keepdims=True)

    gate = jnp.zeros((rows, width), jnp.float32)
    for k in range(ids_ref.shape[0]):
        number = upright(ids_ref[k : k + 1, :].astype(jnp.float32))
        gate += jnp.where(number == expert, upright(gates_ref[k : k + 1, :]), 0.0)
    high = gate.astype(jnp.bfloat16).astype(jnp.float32)
    middle = (gate - high).astype(jnp.bfloat16).astype(jnp.float32)
    low = gate - high - middle
    panel = lax.broadcasted_iota(jnp.int32, (rows, pan_count), 1)
    row = lax.broadcasted_iota(jnp.int32, (rows, pan_count), 0) - text_rows
    past = row - panel * panel_rows
    mine = (past >= 0) & (past < panel_rows)
    target = jnp.sum(
        jnp.where(mine, target_ref[...].astype(jnp.float32), 0.0), axis=1, keepdims=True
    )
    within = jnp.sum(jnp.where(mine, past.astype(jnp.float32), 0.0), axis=1, keepdims=True)
    owner, seq = jnp.zeros_like(target), jnp.zeros_like(target)
    for i in range(1, experts):
        passed = jnp.where(target >= i * pan_count, 1.0, 0.0)
        owner += passed
        if i % expert_count == 0:
            seq += passed
    place = (target - owner * pan_count) * panel_rows + within
    tags = jnp.where(term == 0, high, jnp.where(term == 1, middle, jnp.where(term == 2, low, 0.0)))
    tags = jnp.where(lane == 3 * experts, seq, jnp.where(lane == 3 * experts + 1, place, tags))
    out_ref[:, wide:] = tags.astype(jnp.bfloat16)
    for copy in copies:
        copy.wait()


def pack_call(text_tokens, panels, panel_target, expert_ids, gate_weights, experts, expert_count):
    rows, wide = expert_ids.shape[0], text_tokens.shape[1]
    width = (3 * experts + 2 + 127) // 128 * 128
    here, far = pl.BlockSpec(memory_space=pltpu.VMEM), pl.BlockSpec(memory_space=pltpu.HBM)
    return pl.pallas_call(
        functools.partial(pack_kernel, experts, expert_count),
        in_specs=[far] * 5,
        out_specs=here,
        out_shape=pltpu.VMEM((rows, wide + width), jnp.bfloat16),
        scratch_shapes=[
            pltpu.VMEM((1, panel_target.shape[0]), jnp.int32),
            pltpu.VMEM(expert_ids.shape[::-1], jnp.int32),
            pltpu.VMEM(gate_weights.shape[::-1], jnp.float32),
            pltpu.SemaphoreType.DMA((5,)),
        ],
        compiler_params=pltpu.CompilerParams(vmem_limit_bytes=14 * 1024 * 1024),
    )(
        distant(text_tokens),
        distant(panels.reshape(-1, wide)),
        distant(panel_target[None, :]),
        distant(expert_ids.T),
        distant(gate_weights.T),
    )


def hidden_kernel(places, rows, chunk, fetch, unroll, *refs):
    x_refs, refs = refs[: len(places)], refs[len(places) :]
    if fetch == "gate_up":
        far_ref, out_ref, w_ref, x_all, sems = refs
    elif fetch == "down":
        w_ref, _, far_ref, out_ref, _, down_ref, x_all, sems = refs
    else:
        w_ref, _, out_ref, x_all = refs[0], refs[1], refs[2], refs[-1]
    ff, wide = w_ref.shape[2:]
    whole, rest = divmod(ff, chunk)

    def fetched(i, width):
        part = pl.ds(pl.multiple_of(i * chunk, chunk), width)
        return pltpu.make_async_copy(far_ref.at[0, :, part], w_ref.at[0, :, part], sems.at[i])

    if fetch == "gate_up":
        for i in range(whole):
            fetched(i, chunk).start()
        if rest:
            fetched(whole, rest).start()
    if fetch == "down":
        pltpu.make_async_copy(far_ref, down_ref, sems.at[0]).start()
    for i, at in enumerate(places):
        x_all[i * rows : (i + 1) * rows, :] = x_refs[i][:, :wide]
        out_ref[at : at + rows, ff:] = x_refs[i][:, wide:]

    def step(i, width):
        if fetch == "gate_up":
            fetched(i, width).wait()
        part = pl.ds(chunk_start(i, chunk), width)
        weight = w_ref[0, :, part, :].reshape(2 * width, wide)
        both = lax.dot_general(
            x_all[...], weight, (((1,), (1,)), ((), ())), preferred_element_type=jnp.float32
        )
        gate, up = both[:, :width], both[:, width:]
        gate = 0.5 * gate
        hidden = (gate * (1.0 + jnp.tanh(gate)) * up).astype(out_ref.dtype)
        for i, at in enumerate(places):
            out_ref[at : at + rows, part] = hidden[i * rows : (i + 1) * rows]

    def full_step(i):
        step(i, chunk)

    steps(whole, unroll, full_step)
    if rest:
        step(whole, rest)
    if fetch == "down":
        pltpu.make_async_copy(far_ref, down_ref, sems.at[0]).wait()


def hidden_call(
    blocks, places, gate_up_weight, hidden, all_rows, down_weight=None, last=False, unroll=False
):
    rows, width = blocks[0].shape
    ff, wide = gate_up_weight.shape[2:]
    count = len(blocks)
    chunk = 256
    here, far = pl.BlockSpec(memory_space=pltpu.VMEM), pl.BlockSpec(memory_space=pltpu.HBM)
    args, in_specs = [kept(block) for block in blocks], [here] * count
    out_shape, aliases = [pltpu.VMEM((all_rows, ff + width - wide), jnp.bfloat16)], {}
    scratch = [pltpu.VMEM((count * rows, wide), jnp.bfloat16)]
    fetch = None
    if hidden is None:
        fetch = "gate_up"
        args, in_specs = args + [distant(gate_up_weight)], in_specs + [far]
        out_shape.append(pltpu.VMEM(gate_up_weight.shape, gate_up_weight.dtype))
        scratch.append(pltpu.SemaphoreType.DMA((pl.cdiv(ff, chunk),)))
    else:
        args, in_specs = args + [kept(gate_up_weight), kept(hidden)], in_specs + [here, here]
        aliases = {count + 1: 0}
        if not last:
            out_shape.append(pltpu.VMEM(gate_up_weight.shape, gate_up_weight.dtype))
            aliases[count] = 1
        if down_weight is not None:
            fetch = "down"
            args, in_specs = args + [distant(down_weight)], in_specs + [far]
            out_shape.append(pltpu.VMEM(down_weight.shape, down_weight.dtype))
            scratch.append(pltpu.SemaphoreType.DMA((1,)))
    return pl.pallas_call(
        functools.partial(hidden_kernel, tuple(places), rows, chunk, fetch, unroll),
        in_specs=in_specs,
        out_specs=[here] * len(out_shape),
        out_shape=out_shape,
        scratch_shapes=scratch,
        input_output_aliases=aliases,
        compiler_params=pltpu.CompilerParams(vmem_limit_bytes=14 * 1024 * 1024),
        cost_estimate=pl.CostEstimate(
            flops=4 * count * rows * wide * ff,
            bytes_accessed=4 * ff * wide + 2 * count * rows * (wide + ff),
            transcendentals=count * rows * ff,
        ),
    )(*args)


def down_kernel(
    groups, rows, text_rows, seq_count, experts, chunk, unroll, places_ref, hidden_ref, w_ref, *refs
):
    out_refs, (column, picked, scale) = refs[:-3], refs[-3:]
    slots = [slot for group in groups for slot in group]
    image_rows = rows - text_rows
    slot_total = hidden_ref.shape[0] // rows
    ff = w_ref.shape[1]
    width = hidden_ref.shape[1] - ff
    expert = places_ref[0]
    lane = lax.broadcasted_iota(jnp.int32, (1, width), 1)
    is_gate = (lane == expert) | (lane == expert + experts) | (lane == expert + 2 * experts)
    place_of = jnp.where(lane == 3 * experts, float(image_rows), 0.0)
    place_of = jnp.where(lane == 3 * experts + 1, 1.0, place_of)
    wanted = lax.broadcasted_iota(jnp.int32, (1, image_rows), 1)
    for j, slot in enumerate(slots):
        at = slot * rows
        picked[j * rows : j * rows + text_rows, :] = hidden_ref[at : at + text_rows, :ff]
        for z in range(seq_count):
            source = places_ref[1 + slot_total + slot * seq_count + z]
            start = pl.multiple_of(source * rows + text_rows, 16)
            column[z * image_rows : (z + 1) * image_rows, :] = hidden_ref[
                pl.ds(start, image_rows), :
            ]
        place = column[:, ff:].astype(jnp.float32) * place_of
        place = jnp.sum(place, axis=1, keepdims=True)
        first = places_ref[1 + slot] * image_rows
        match = jnp.where(place == (wanted + first).astype(jnp.float32), 1.0, 0.0)
        rows_here = lax.dot_general(
            match.astype(jnp.bfloat16),
            column[:, :ff],
            (((0,), (0,)), ((), ())),
            preferred_element_type=jnp.float32,
        )
        picked[j * rows + text_rows : (j + 1) * rows, :] = rows_here.astype(jnp.bfloat16)
        gates = jnp.where(is_gate, hidden_ref[at : at + rows, ff:].astype(jnp.float32), 0.0)
        scale[j * rows : (j + 1) * rows, :] = jnp.sum(gates, axis=1, keepdims=True)

    def step(i):
        part = pl.ds(chunk_start(i, chunk), chunk)
        result = jnp.dot(picked[...], w_ref[0, :, part], preferred_element_type=jnp.float32)
        scaled = result.astype(jnp.bfloat16).astype(jnp.float32) * scale[...]
        scaled = scaled.astype(jnp.bfloat16)
        start = 0
        for out_ref in out_refs:
            out_ref[:, part] = scaled[start : start + out_ref.shape[0]]
            start += out_ref.shape[0]

    steps(w_ref.shape[2] // chunk, unroll, step)


def down_call(
    hidden, places, down_weight, groups, rows, text_rows, seq_count, experts, unroll
):
    _, ff, wide = down_weight.shape
    total = sum(len(group) for group in groups) * rows
    here = pl.BlockSpec(memory_space=pltpu.VMEM)
    return pl.pallas_call(
        functools.partial(
            down_kernel, groups, rows, text_rows, seq_count, experts, 512, unroll
        ),
        grid_spec=pltpu.PrefetchScalarGridSpec(
            num_scalar_prefetch=1,
            grid=(1,),
            in_specs=[here] * 2,
            out_specs=[here] * len(groups),
            scratch_shapes=[
                pltpu.VMEM((seq_count * (rows - text_rows), hidden.shape[1]), jnp.bfloat16),
                pltpu.VMEM((total, ff), jnp.bfloat16),
                pltpu.VMEM((total, 1), jnp.float32),
            ],
        ),
        out_shape=[pltpu.VMEM((len(group) * rows, wide), jnp.bfloat16) for group in groups],
        compiler_params=pltpu.CompilerParams(vmem_limit_bytes=14 * 1024 * 1024),
        cost_estimate=pl.CostEstimate(
            flops=2 * total * wide * ff,
            bytes_accessed=2 * ff * wide + 2 * total * wide,
            transcendentals=0,
        ),
    )(places, kept(hidden), kept(down_weight))


def add_up(*parts):
    total = parts[0].astype(jnp.float32)
    for part in parts[1:]:
        total = total + part.astype(jnp.float32)
    return total.astype(jnp.bfloat16)


def ring_shards(
    text_tokens, panels, panel_target, expert_ids, gate_weights, gate_up_weight, down_weight
):
    seq_count, expert_count = lax.axis_size("seq"), lax.axis_size("expert")
    ring = Ring(seq_count, expert_count)
    text_rows, tok_count = text_tokens.shape[0], expert_ids.shape[0]
    me = lax.axis_index(AXES)

    def along(array):
        return lax.ppermute(array, AXES, ring.step())

    def across(array):
        return lax.ppermute(array, AXES, ring.swap())

    own = pack_call(
        text_tokens, panels, panel_target, expert_ids, gate_weights, ring.devices, expert_count
    )
    seq_of = ring.owner_of // expert_count
    numbers = np.arange(ring.devices, dtype=np.int32)[:, None]
    places = np.concatenate([numbers, seq_of, ring.sources_of.reshape(ring.devices, -1)], axis=1)
    places = jnp.asarray(places)[me]

    all_rows = ring.slot_count * tok_count

    def tied(*values):
        return lax.optimization_barrier(values)

    def rows_of(*slots):
        return [slot * tok_count for slot in slots]

    lead = along(own)
    other = across(own)
    own, places = tied(own, places)
    hidden, gate_up = hidden_call([own, other], rows_of(0, 1), gate_up_weight, None, all_rows)
    trail = along(other)
    hidden, lead = tied(hidden, lead)
    hidden, trail = tied(hidden, trail)
    swapped = swapped_rows = None
    for s in range(1, ring.half):
        next_lead = along(lead)
        lead_across = across(lead)
        if swapped:
            hidden, gate_up = hidden_call(swapped, swapped_rows, gate_up, hidden, all_rows)
            hidden, trail = tied(hidden, trail)
        next_trail = along(trail) if s + 1 < ring.half else None
        trail_across = across(trail)
        extra = down_weight if s == 1 else None
        hidden, gate_up, *down = hidden_call(
            [lead, trail], rows_of(4 * s, 4 * s + 1), gate_up, hidden, all_rows, extra,
            unroll=s + 1 == ring.half,
        )
        if down:
            (down_here,) = down
        hidden, lead, lead_across, trail_across = tied(
            hidden, next_lead, lead_across, trail_across
        )
        trail = next_trail
        swapped, swapped_rows = [lead_across, trail_across], rows_of(4 * s + 3, 4 * s + 2)
    hidden, gate_up = hidden_call(swapped, swapped_rows, gate_up, hidden, all_rows, unroll=True)
    far = [lead, across(lead)]
    (hidden,) = hidden_call(
        far, rows_of(2, 3), gate_up, hidden, all_rows, last=True, unroll=True
    )

    def outputs(hidden, *groups, unroll=False):
        return down_call(
            hidden, places, down_here, groups, tok_count, text_rows, seq_count, ring.devices, unroll
        )

    def for_other(hidden, s):
        groups = ((4 * s + 1,), (4 * s,)) if s else ((1,),)
        first, *rest = outputs(hidden, *groups, unroll=s + 2 >= ring.half)
        first, hidden = tied(first, hidden)
        return [first, *rest], hidden

    def for_own(hidden, s):
        groups = ((4 * s + 2,), (4 * s + 3,)) if s else ((0,),)
        first, *rest = outputs(hidden, *groups, unroll=s + 1 >= ring.half)
        first, hidden = tied(first, hidden)
        return [first, *rest], hidden

    def sent(hidden, *parts):
        total, hidden = tied(add_up(*parts), hidden)
        return along(total), hidden

    mine, others = outputs(hidden, (2,), (3,), unroll=True)
    mine, hidden = tied(mine, hidden)
    swapped, hidden = for_other(hidden, ring.half - 1)
    swapped = [across(array) for array in swapped]
    lead, hidden = sent(hidden, mine, across(others))
    mine, hidden = for_own(hidden, ring.half - 1)
    trail, hidden = sent(hidden, mine[1], swapped[1])
    for s in range(ring.half - 1, 0, -1):
        next_swapped, hidden = for_other(hidden, s - 1)
        if s > 1:
            next_swapped = [across(array) for array in next_swapped]
        lead, hidden = sent(hidden, mine[0], swapped[0], lead)
        mine, hidden = for_own(hidden, s - 1)
        swapped = next_swapped
        if s > 1:
            trail, hidden = sent(hidden, mine[1], swapped[1], trail)
    return add_up(mine[0], across(add_up(swapped[0], trail)), lead)


def solution(mesh):
    placed = (
        P(("groups", "seq", "expert"), "tensor"),
        P(("groups", "seq", "expert"), None, "tensor"),
        P(("groups", "seq", "expert")),
        P(("groups", "seq", "expert"), None),
        P(("groups", "seq", "expert"), None),
        P(("seq", "expert"), None, "tensor", None),
        P(("seq", "expert"), "tensor", None),
    )

    def chosen(*args):
        seq_count, expert_count = mesh.shape["seq"], mesh.shape["expert"]
        owners = seq_count * expert_count
        tok_count, top_count = args[3].shape[0] // (mesh.shape["groups"] * owners), args[3].shape[1]
        experts_all = args[5].shape[0]
        slot_rows = experts_all * slot_capacity(tok_count, top_count, experts_all)
        dense = owners * tok_count <= 2 * slot_rows
        ring = dense and mesh.shape["tensor"] == 1 and expert_count == 4 and experts_all == owners
        ring = ring and seq_count > 2
        body = ring_shards if ring else slot_shards
        return jax.shard_map(
            body,
            mesh=mesh,
            in_specs=placed,
            out_specs=P(("groups", "seq", "expert"), "tensor"),
            check_vma=False,
        )(*args)

    return chosen
```

profile of v0, /device:TPU:0, one launch (start us, length us, event | category | flops | bytes accessed | tf_op | source)
XLA Modules:
  0.0 157.3 jit_solution(14319533912638046993)
XLA Ops:
  1.8 2.6 %collective-permute-start.1 = (bf16[160,2688]{1,0:T(8,128)(2,1)S(1)}, bf16[160,2688]{1,0:T(8,128)(2,1)S(1)}, u32[]{:S(2)}, u32[]{:S(2)}) collective-permute-start(bf16[160,2688]{1,0:T(8,128)(2,1)S(1)} %shard_map.82.refs_0_), channel_id=1, source_target_pairs={{0,4},{1,3},{2,0},{3,7},{4,8},{5,1},{6,2},{7,11},{8,12},{9,5},{10,... | collective-permute-start | bytes 2580488 | tf_op jit(solution)/shard_map/ppermute | solution.py:464
  4.4 2.3 %collective-permute-start.2 = (bf16[160,2688]{1,0:T(8,128)(2,1)S(1)}, bf16[160,2688]{1,0:T(8,128)(2,1)S(1)}, u32[]{:S(2)}, u32[]{:S(2)}) collective-permute-start(bf16[160,2688]{1,0:T(8,128)(2,1)S(1)} %collective-permute-done.refs_1_), channel_id=1, source_target_pairs={{0,4},{1,3},{2,0},{3,7},{4,8},{5,1},{6,2},{7,11},{8,12},{9,5},{10,... | collective-permute-start | bytes 2580488 | tf_op jit(solution)/shard_map/ppermute | solution.py:464
  7.5 7.7 %shard_map.83 = (bf16[2560,1536]{1,0:T(8,128)(2,1)S(1)}, bf16[1,2,1408,2560]{3,2,1,0:T(8,128)(2,1)S(1)}) custom-call(bf16[160,2688]{1,0:T(8,128)(2,1)S(1)} %shard_map.82.refs_0_, bf16[160,2688]{1,0:T(8,128)(2,1)S(1)} %collective-permute-done.refs_1_, bf16[1,2,1408,2560]{3,2,1,0:T(8,128)(2,1)} %refs_2_.1), custom_call_target="tpu_custom_call" | custom-call | flops 4613734400 | bytes 16957440 | tf_op jit(solution)/shard_map/pallas_call | solution.py:350
  15.2 2.0 %collective-permute-start.3 = (bf16[160,2688]{1,0:T(8,128)(2,1)S(1)}, bf16[160,2688]{1,0:T(8,128)(2,1)S(1)}, u32[]{:S(2)}, u32[]{:S(2)}) collective-permute-start(bf16[160,2688]{1,0:T(8,128)(2,1)S(1)} %collective-permute-done.1.refs_0_), channel_id=1, source_target_pairs={{0,4},{1,3},{2,0},{3,7},{4,8},{5,1},{6,2},{7,11},{8,12},{9,5},{10,... | collective-permute-start | bytes 2580488 | tf_op jit(solution)/shard_map/ppermute | solution.py:464
  17.2 7.1 %collective-permute-done.2.refs_1_ = bf16[160,2688]{1,0:T(8,128)(2,1)S(1)} collective-permute-done((bf16[160,2688]{1,0:T(8,128)(2,1)S(1)}, bf16[160,2688]{1,0:T(8,128)(2,1)S(1)}, u32[]{:S(2)}, u32[]{:S(2)}) %collective-permute-start.2) | collective-permute-done | bytes 860192 | tf_op jit(solution)/shard_map/ppermute | solution.py:464
  24.3 2.1 %collective-permute-start.6 = (bf16[160,2688]{1,0:T(8,128)(2,1)S(1)}, bf16[160,2688]{1,0:T(8,128)(2,1)S(1)}, u32[]{:S(2)}, u32[]{:S(2)}) collective-permute-start(bf16[160,2688]{1,0:T(8,128)(2,1)S(1)} %collective-permute-done.2.refs_1_), channel_id=1, source_target_pairs={{0,4},{1,3},{2,0},{3,7},{4,8},{5,1},{6,2},{7,11},{8,12},{9,5},{10,... | collective-permute-start | bytes 2580488 | tf_op jit(solution)/shard_map/ppermute | solution.py:464
  26.4 6.0 %shard_map.84 = (bf16[2560,1536]{1,0:T(8,128)(2,1)S(1)}, bf16[1,2,1408,2560]{3,2,1,0:T(8,128)(2,1)S(1)}, bf16[1,1408,2560]{2,1,0:T(8,128)(2,1)S(1)}) custom-call(bf16[160,2688]{1,0:T(8,128)(2,1)S(1)} %collective-permute-done.1.refs_0_, bf16[160,2688]{1,0:T(8,128)(2,1)S(1)} %collective-permute-done.2.refs_1_, ...), custom_call_target="tpu_custom_call", output_to_operand_aliasing={{0}: (3, {}), {1}: (2, {})} | custom-call | flops 4613734400 | bytes 16957440 | tf_op jit(solution)/shard_map/pallas_call | solution.py:350
  33.6 2.1 %collective-permute-start.7 = (bf16[160,2688]{1,0:T(8,128)(2,1)S(1)}, bf16[160,2688]{1,0:T(8,128)(2,1)S(1)}, u32[]{:S(2)}, u32[]{:S(2)}) collective-permute-start(bf16[160,2688]{1,0:T(8,128)(2,1)S(1)} %collective-permute-done.3.refs_0_), channel_id=1, source_target_pairs={{0,4},{1,3},{2,0},{3,7},{4,8},{5,1},{6,2},{7,11},{8,12},{9,5},{10,... | collective-permute-start | bytes 2580488 | tf_op jit(solution)/shard_map/ppermute | solution.py:464
  35.7 6.0 %shard_map.85 = (bf16[2560,1536]{1,0:T(8,128)(2,1)S(1)}, bf16[1,2,1408,2560]{3,2,1,0:T(8,128)(2,1)S(1)}) custom-call(bf16[160,2688]{1,0:T(8,128)(2,1)S(1)} %collective-permute-done.4.refs_0_, bf16[160,2688]{1,0:T(8,128)(2,1)S(1)} %collective-permute-done.5.refs_1_, ...), custom_call_target="tpu_custom_call", output_to_operand_aliasing={{0}: (3, {}), {1}: (2, {})} | custom-call | flops 4613734400 | bytes 16957440 | tf_op jit(solution)/shard_map/pallas_call | solution.py:350
  42.8 2.1 %collective-permute-start.10 = (bf16[160,2688]{1,0:T(8,128)(2,1)S(1)}, bf16[160,2688]{1,0:T(8,128)(2,1)S(1)}, u32[]{:S(2)}, u32[]{:S(2)}) collective-permute-start(bf16[160,2688]{1,0:T(8,128)(2,1)S(1)} %collective-permute-done.6.refs_1_), channel_id=1, source_target_pairs={{0,4},{1,3},{2,0},{3,7},{4,8},{5,1},{6,2},{7,11},{8,12},{9,5},{10,... | collective-permute-start | bytes 2580488 | tf_op jit(solution)/shard_map/ppermute | solution.py:464
  44.9 6.0 %shard_map.86 = (bf16[2560,1536]{1,0:T(8,128)(2,1)S(1)}, bf16[1,2,1408,2560]{3,2,1,0:T(8,128)(2,1)S(1)}) custom-call(bf16[160,2688]{1,0:T(8,128)(2,1)S(1)} %collective-permute-done.3.refs_0_, bf16[160,2688]{1,0:T(8,128)(2,1)S(1)} %collective-permute-done.6.refs_1_, ...), custom_call_target="tpu_custom_call", output_to_operand_aliasing={{0}: (3, {}), {1}: (2, {})} | custom-call | flops 4613734400 | bytes 16957440 | tf_op jit(solution)/shard_map/pallas_call | solution.py:350
  52.0 2.1 %collective-permute-start.11 = (bf16[160,2688]{1,0:T(8,128)(2,1)S(1)}, bf16[160,2688]{1,0:T(8,128)(2,1)S(1)}, u32[]{:S(2)}, u32[]{:S(2)}) collective-permute-start(bf16[160,2688]{1,0:T(8,128)(2,1)S(1)} %collective-permute-done.7.refs_0_), channel_id=1, source_target_pairs={{0,4},{1,3},{2,0},{3,7},{4,8},{5,1},{6,2},{7,11},{8,12},{9,5},{10,... | collective-permute-start | bytes 2580488 | tf_op jit(solution)/shard_map/ppermute | solution.py:464
  54.1 6.2 %shard_map.87 = (bf16[2560,1536]{1,0:T(8,128)(2,1)S(1)}, bf16[1,2,1408,2560]{3,2,1,0:T(8,128)(2,1)S(1)}) custom-call(bf16[160,2688]{1,0:T(8,128)(2,1)S(1)} %collective-permute-done.8.refs_0_, bf16[160,2688]{1,0:T(8,128)(2,1)S(1)} %collective-permute-done.9.refs_1_, ...), custom_call_target="tpu_custom_call", output_to_operand_aliasing={{0}: (3, {}), {1}: (2, {})} | custom-call | flops 4613734400 | bytes 16957440 | tf_op jit(solution)/shard_map/pallas_call | solution.py:350
  61.2 4.9 %shard_map.88 = (bf16[2560,1536]{1,0:T(8,128)(2,1)S(1)}, bf16[1,2,1408,2560]{3,2,1,0:T(8,128)(2,1)S(1)}) custom-call(bf16[160,2688]{1,0:T(8,128)(2,1)S(1)} %collective-permute-done.7.refs_0_, bf16[160,2688]{1,0:T(8,128)(2,1)S(1)} %collective-permute-done.10.refs_1_, ...), custom_call_target="tpu_custom_call", output_to_operand_aliasing={{0}: (3, {}), {1}: (2, {})} | custom-call | flops 4613734400 | bytes 16957440 | tf_op jit(solution)/shard_map/pallas_call | solution.py:350
  66.1 4.4 %collective-permute-done.11.refs_0_ = bf16[160,2688]{1,0:T(8,128)(2,1)S(1)} collective-permute-done((bf16[160,2688]{1,0:T(8,128)(2,1)S(1)}, bf16[160,2688]{1,0:T(8,128)(2,1)S(1)}, u32[]{:S(2)}, u32[]{:S(2)}) %collective-permute-start.11) | collective-permute-done | bytes 860192 | tf_op jit(solution)/shard_map/ppermute | solution.py:464
  70.4 4.9 %shard_map.89 = (bf16[2560,1536]{1,0:T(8,128)(2,1)S(1)}, bf16[1,2,1408,2560]{3,2,1,0:T(8,128)(2,1)S(1)}) custom-call(bf16[160,2688]{1,0:T(8,128)(2,1)S(1)} %collective-permute-done.12.refs_0_, bf16[160,2688]{1,0:T(8,128)(2,1)S(1)} %collective-permute-done.13.refs_1_, ...), custom_call_target="tpu_custom_call", output_to_operand_aliasing={{0}: (3, {}), {1}: (2, {})} | custom-call | flops 4613734400 | bytes 16957440 | tf_op jit(solution)/shard_map/pallas_call | solution.py:350
  75.3 4.9 %shard_map.90.hidden_ref = bf16[2560,1536]{1,0:T(8,128)(2,1)S(1)} custom-call(bf16[160,2688]{1,0:T(8,128)(2,1)S(1)} %collective-permute-done.11.refs_0_, bf16[160,2688]{1,0:T(8,128)(2,1)S(1)} %collective-permute-done.14.refs_1_, bf16[1,2,1408,2560]{3,2,1,0:T(8,128)(2,1)S(1)} %get-tuple-element.121.refs_2_, ...), custom_call_target="tpu_custom_call", output_to_operand_aliasing={{}: (3, {})} | custom-call | flops 4613734400 | bytes 16957440 | tf_op jit(solution)/shard_map/pallas_call | solution.py:350
  80.2 4.1 %shard_map.91 = (bf16[160,2560]{1,0:T(8,128)(2,1)S(1)}, bf16[160,2560]{1,0:T(8,128)(2,1)S(1)}) custom-call(s32[81]{0:T(128)S(1)} %dynamic-slice_bitcast_fusion.places_ref, bf16[2560,1536]{1,0:T(8,128)(2,1)S(1)} %shard_map.90.hidden_ref, bf16[1,1408,2560]{2,1,0:T(8,128)(2,1)S(1)} %get-tuple-element.123.w_ref), custom_call_target="tpu_custom_call" | custom-call | flops 2306867200 | bytes 8847360 | tf_op jit(solution)/shard_map/pallas_call | solution.py:423
  84.9 3.9 %shard_map.92 = (bf16[160,2560]{1,0:T(8,128)(2,1)S(1)}, bf16[160,2560]{1,0:T(8,128)(2,1)S(1)}) custom-call(s32[81]{0:T(128)S(1)} %dynamic-slice_bitcast_fusion.places_ref, bf16[2560,1536]{1,0:T(8,128)(2,1)S(1)} %shard_map.90.hidden_ref, bf16[1,1408,2560]{2,1,0:T(8,128)(2,1)S(1)} %get-tuple-element.123.w_ref), custom_call_target="tpu_custom_call" | custom-call | flops 2306867200 | bytes 8847360 | tf_op jit(solution)/shard_map/pallas_call | solution.py:423
  89.6 2.2 %collective-permute-start.17 = (bf16[160,2560]{1,0:T(8,128)(2,1)S(1)}, bf16[160,2560]{1,0:T(8,128)(2,1)S(1)}, u32[]{:S(2)}, u32[]{:S(2)}) collective-permute-start(bf16[160,2560]{1,0:T(8,128)(2,1)S(1)} %add_convert_fusion.8), channel_id=1, source_target_pairs={{0,4},{1,3},{2,0},{3,7},{4,8},{5,1},{6,2},{7,11},{8,12},{9,5},{10,... | collective-permute-start | bytes 2457608 | tf_op jit(solution)/shard_map/ppermute | solution.py:464
  91.7 3.9 %shard_map.93 = (bf16[160,2560]{1,0:T(8,128)(2,1)S(1)}, bf16[160,2560]{1,0:T(8,128)(2,1)S(1)}) custom-call(s32[81]{0:T(128)S(1)} %dynamic-slice_bitcast_fusion.places_ref, bf16[2560,1536]{1,0:T(8,128)(2,1)S(1)} %shard_map.90.hidden_ref, bf16[1,1408,2560]{2,1,0:T(8,128)(2,1)S(1)} %get-tuple-element.123.w_ref), custom_call_target="tpu_custom_call" | custom-call | flops 2306867200 | bytes 8847360 | tf_op jit(solution)/shard_map/pallas_call | solution.py:423
  95.8 3.9 %shard_map.94 = (bf16[160,2560]{1,0:T(8,128)(2,1)S(1)}, bf16[160,2560]{1,0:T(8,128)(2,1)S(1)}) custom-call(s32[81]{0:T(128)S(1)} %dynamic-slice_bitcast_fusion.places_ref, bf16[2560,1536]{1,0:T(8,128)(2,1)S(1)} %shard_map.90.hidden_ref, bf16[1,1408,2560]{2,1,0:T(8,128)(2,1)S(1)} %get-tuple-element.123.w_ref), custom_call_target="tpu_custom_call" | custom-call | flops 2306867200 | bytes 8847360 | tf_op jit(solution)/shard_map/pallas_call | solution.py:423
  102.3 2.2 %collective-permute-start.20 = (bf16[160,2560]{1,0:T(8,128)(2,1)S(1)}, bf16[160,2560]{1,0:T(8,128)(2,1)S(1)}, u32[]{:S(2)}, u32[]{:S(2)}) collective-permute-start(bf16[160,2560]{1,0:T(8,128)(2,1)S(1)} %add_convert_fusion.7), channel_id=1, source_target_pairs={{0,4},{1,3},{2,0},{3,7},{4,8},{5,1},{6,2},{7,11},{8,12},{9,5},{10,... | collective-permute-start | bytes 2457608 | tf_op jit(solution)/shard_map/ppermute | solution.py:464
  104.5 4.7 %shard_map.95 = (bf16[160,2560]{1,0:T(8,128)(2,1)S(1)}, bf16[160,2560]{1,0:T(8,128)(2,1)S(1)}) custom-call(s32[81]{0:T(128)S(1)} %dynamic-slice_bitcast_fusion.places_ref, bf16[2560,1536]{1,0:T(8,128)(2,1)S(1)} %shard_map.90.hidden_ref, bf16[1,1408,2560]{2,1,0:T(8,128)(2,1)S(1)} %get-tuple-element.123.w_ref), custom_call_target="tpu_custom_call" | custom-call | flops 2306867200 | bytes 8847360 | tf_op jit(solution)/shard_map/pallas_call | solution.py:423
  109.2 3.0 %collective-permute-done.22 = bf16[160,2560]{1,0:T(8,128)(2,1)S(1)} collective-permute-done((bf16[160,2560]{1,0:T(8,128)(2,1)S(1)}, bf16[160,2560]{1,0:T(8,128)(2,1)S(1)}, u32[]{:S(2)}, u32[]{:S(2)}) %collective-permute-start.22) | collective-permute-done | bytes 819232 | tf_op jit(solution)/shard_map/ppermute | solution.py:464
  112.6 4.7 %shard_map.96 = (bf16[160,2560]{1,0:T(8,128)(2,1)S(1)}, bf16[160,2560]{1,0:T(8,128)(2,1)S(1)}) custom-call(s32[81]{0:T(128)S(1)} %dynamic-slice_bitcast_fusion.places_ref, bf16[2560,1536]{1,0:T(8,128)(2,1)S(1)} %shard_map.90.hidden_ref, bf16[1,1408,2560]{2,1,0:T(8,128)(2,1)S(1)} %get-tuple-element.123.w_ref), custom_call_target="tpu_custom_call" | custom-call | flops 2306867200 | bytes 8847360 | tf_op jit(solution)/shard_map/pallas_call | solution.py:423
  123.2 4.7 %shard_map.97 = (bf16[160,2560]{1,0:T(8,128)(2,1)S(1)}, bf16[160,2560]{1,0:T(8,128)(2,1)S(1)}) custom-call(s32[81]{0:T(128)S(1)} %dynamic-slice_bitcast_fusion.places_ref, bf16[2560,1536]{1,0:T(8,128)(2,1)S(1)} %shard_map.90.hidden_ref, bf16[1,1408,2560]{2,1,0:T(8,128)(2,1)S(1)} %get-tuple-element.123.w_ref), custom_call_target="tpu_custom_call" | custom-call | flops 2306867200 | bytes 8847360 | tf_op jit(solution)/shard_map/pallas_call | solution.py:423
  131.8 3.2 %shard_map.98 = bf16[160,2560]{1,0:T(8,128)(2,1)S(1)} custom-call(s32[81]{0:T(128)S(1)} %dynamic-slice_bitcast_fusion.places_ref, bf16[2560,1536]{1,0:T(8,128)(2,1)S(1)} %shard_map.90.hidden_ref, bf16[1,1408,2560]{2,1,0:T(8,128)(2,1)S(1)} %get-tuple-element.123.w_ref), custom_call_target="tpu_custom_call" | custom-call | flops 1153433600 | bytes 8028160 | tf_op jit(solution)/shard_map/pallas_call | solution.py:423
  135.0 3.6 %collective-permute-done.24 = bf16[160,2560]{1,0:T(8,128)(2,1)S(1)} collective-permute-done((bf16[160,2560]{1,0:T(8,128)(2,1)S(1)}, bf16[160,2560]{1,0:T(8,128)(2,1)S(1)}, u32[]{:S(2)}, u32[]{:S(2)}) %collective-permute-start.24) | collective-permute-done | bytes 819232 | tf_op jit(solution)/shard_map/ppermute | solution.py:464
  140.5 6.8 %collective-permute-done.27 = bf16[160,2560]{1,0:T(8,128)(2,1)S(1)} collective-permute-done((bf16[160,2560]{1,0:T(8,128)(2,1)S(1)}, bf16[160,2560]{1,0:T(8,128)(2,1)S(1)}, u32[]{:S(2)}, u32[]{:S(2)}) %collective-permute-start.27) | collective-permute-done | bytes 819232 | tf_op jit(solution)/shard_map/ppermute | solution.py:464
  147.6 3.2 %shard_map.99 = bf16[160,2560]{1,0:T(8,128)(2,1)S(1)} custom-call(s32[81]{0:T(128)S(1)} %dynamic-slice_bitcast_fusion.places_ref, bf16[2560,1536]{1,0:T(8,128)(2,1)S(1)} %shard_map.90.hidden_ref, bf16[1,1408,2560]{2,1,0:T(8,128)(2,1)S(1)} %get-tuple-element.123.w_ref), custom_call_target="tpu_custom_call" | custom-call | flops 1153433600 | bytes 8028160 | tf_op jit(solution)/shard_map/pallas_call | solution.py:423
  150.9 5.2 %collective-permute-done.29 = bf16[160,2560]{1,0:T(8,128)(2,1)S(1)} collective-permute-done((bf16[160,2560]{1,0:T(8,128)(2,1)S(1)}, bf16[160,2560]{1,0:T(8,128)(2,1)S(1)}, u32[]{:S(2)}, u32[]{:S(2)}) %collective-permute-start.29) | collective-permute-done | bytes 819232 | tf_op jit(solution)/shard_map/ppermute | solution.py:464
  (56 shorter events, 24.5 us)
Async XLA Ops:
  1.3 3.2 %collective-permute-start = (bf16[160,2688]{1,0:T(8,128)(2,1)S(1)}, bf16[160,2688]{1,0:T(8,128)(2,1)S(1)}, u32[]{:S(2)}, u32[]{:S(2)}) collective-permute-start(bf16[160,2688]{1,0:T(8,128)(2,1)S(1)} %shard_map.82.refs_0_), channel_id=1, source_target_pairs={{0,1},{1,0},{2,3},{3,2},{4,5},{5,4},{6,7},{7,6},{8,9},{9,8},{10,11... | collective-permute-start | bytes 2580488 | tf_op jit(solution)/shard_map/ppermute | solution.py:467
  1.8 13.4 %collective-permute-start.1 = (bf16[160,2688]{1,0:T(8,128)(2,1)S(1)}, bf16[160,2688]{1,0:T(8,128)(2,1)S(1)}, u32[]{:S(2)}, u32[]{:S(2)}) collective-permute-start(bf16[160,2688]{1,0:T(8,128)(2,1)S(1)} %shard_map.82.refs_0_), channel_id=1, source_target_pairs={{0,4},{1,3},{2,0},{3,7},{4,8},{5,1},{6,2},{7,11},{8,12},{9,5},{10,... | collective-permute-start | bytes 2580488 | tf_op jit(solution)/shard_map/ppermute | solution.py:464
  4.4 19.9 %collective-permute-start.2 = (bf16[160,2688]{1,0:T(8,128)(2,1)S(1)}, bf16[160,2688]{1,0:T(8,128)(2,1)S(1)}, u32[]{:S(2)}, u32[]{:S(2)}) collective-permute-start(bf16[160,2688]{1,0:T(8,128)(2,1)S(1)} %collective-permute-done.refs_1_), channel_id=1, source_target_pairs={{0,4},{1,3},{2,0},{3,7},{4,8},{5,1},{6,2},{7,11},{8,12},{9,5},{10,... | collective-permute-start | bytes 2580488 | tf_op jit(solution)/shard_map/ppermute | solution.py:464
  15.2 18.4 %collective-permute-start.3 = (bf16[160,2688]{1,0:T(8,128)(2,1)S(1)}, bf16[160,2688]{1,0:T(8,128)(2,1)S(1)}, u32[]{:S(2)}, u32[]{:S(2)}) collective-permute-start(bf16[160,2688]{1,0:T(8,128)(2,1)S(1)} %collective-permute-done.1.refs_0_), channel_id=1, source_target_pairs={{0,4},{1,3},{2,0},{3,7},{4,8},{5,1},{6,2},{7,11},{8,12},{9,5},{10,... | collective-permute-start | bytes 2580488 | tf_op jit(solution)/shard_map/ppermute | solution.py:464
  17.2 16.3 %collective-permute-start.4 = (bf16[160,2688]{1,0:T(8,128)(2,1)S(1)}, bf16[160,2688]{1,0:T(8,128)(2,1)S(1)}, u32[]{:S(2)}, u32[]{:S(2)}) collective-permute-start(bf16[160,2688]{1,0:T(8,128)(2,1)S(1)} %collective-permute-done.1.refs_0_), channel_id=1, source_target_pairs={{0,1},{1,0},{2,3},{3,2},{4,5},{5,4},{6,7},{7,6},{8,9},{9,8},{10,11... | collective-permute-start | bytes 2580488 | tf_op jit(solution)/shard_map/ppermute | solution.py:467
  24.3 9.2 %collective-permute-start.5 = (bf16[160,2688]{1,0:T(8,128)(2,1)S(1)}, bf16[160,2688]{1,0:T(8,128)(2,1)S(1)}, u32[]{:S(2)}, u32[]{:S(2)}) collective-permute-start(bf16[160,2688]{1,0:T(8,128)(2,1)S(1)} %collective-permute-done.2.refs_1_), channel_id=1, source_target_pairs={{0,1},{1,0},{2,3},{3,2},{4,5},{5,4},{6,7},{7,6},{8,9},{9,8},{10,11... | collective-permute-start | bytes 2580488 | tf_op jit(solution)/shard_map/ppermute | solution.py:467
  24.3 18.4 %collective-permute-start.6 = (bf16[160,2688]{1,0:T(8,128)(2,1)S(1)}, bf16[160,2688]{1,0:T(8,128)(2,1)S(1)}, u32[]{:S(2)}, u32[]{:S(2)}) collective-permute-start(bf16[160,2688]{1,0:T(8,128)(2,1)S(1)} %collective-permute-done.2.refs_1_), channel_id=1, source_target_pairs={{0,4},{1,3},{2,0},{3,7},{4,8},{5,1},{6,2},{7,11},{8,12},{9,5},{10,... | collective-permute-start | bytes 2580488 | tf_op jit(solution)/shard_map/ppermute | solution.py:464
  33.6 18.4 %collective-permute-start.7 = (bf16[160,2688]{1,0:T(8,128)(2,1)S(1)}, bf16[160,2688]{1,0:T(8,128)(2,1)S(1)}, u32[]{:S(2)}, u32[]{:S(2)}) collective-permute-start(bf16[160,2688]{1,0:T(8,128)(2,1)S(1)} %collective-permute-done.3.refs_0_), channel_id=1, source_target_pairs={{0,4},{1,3},{2,0},{3,7},{4,8},{5,1},{6,2},{7,11},{8,12},{9,5},{10,... | collective-permute-start | bytes 2580488 | tf_op jit(solution)/shard_map/ppermute | solution.py:464
  35.7 16.3 %collective-permute-start.8 = (bf16[160,2688]{1,0:T(8,128)(2,1)S(1)}, bf16[160,2688]{1,0:T(8,128)(2,1)S(1)}, u32[]{:S(2)}, u32[]{:S(2)}) collective-permute-start(bf16[160,2688]{1,0:T(8,128)(2,1)S(1)} %collective-permute-done.3.refs_0_), channel_id=1, source_target_pairs={{0,1},{1,0},{2,3},{3,2},{4,5},{5,4},{6,7},{7,6},{8,9},{9,8},{10,11... | collective-permute-start | bytes 2580488 | tf_op jit(solution)/shard_map/ppermute | solution.py:467
  42.8 9.2 %collective-permute-start.9 = (bf16[160,2688]{1,0:T(8,128)(2,1)S(1)}, bf16[160,2688]{1,0:T(8,128)(2,1)S(1)}, u32[]{:S(2)}, u32[]{:S(2)}) collective-permute-start(bf16[160,2688]{1,0:T(8,128)(2,1)S(1)} %collective-permute-done.6.refs_1_), channel_id=1, source_target_pairs={{0,1},{1,0},{2,3},{3,2},{4,5},{5,4},{6,7},{7,6},{8,9},{9,8},{10,11... | collective-permute-start | bytes 2580488 | tf_op jit(solution)/shard_map/ppermute | solution.py:467
  42.8 18.4 %collective-permute-start.10 = (bf16[160,2688]{1,0:T(8,128)(2,1)S(1)}, bf16[160,2688]{1,0:T(8,128)(2,1)S(1)}, u32[]{:S(2)}, u32[]{:S(2)}) collective-permute-start(bf16[160,2688]{1,0:T(8,128)(2,1)S(1)} %collective-permute-done.6.refs_1_), channel_id=1, source_target_pairs={{0,4},{1,3},{2,0},{3,7},{4,8},{5,1},{6,2},{7,11},{8,12},{9,5},{10,... | collective-permute-start | bytes 2580488 | tf_op jit(solution)/shard_map/ppermute | solution.py:464
  52.0 18.4 %collective-permute-start.11 = (bf16[160,2688]{1,0:T(8,128)(2,1)S(1)}, bf16[160,2688]{1,0:T(8,128)(2,1)S(1)}, u32[]{:S(2)}, u32[]{:S(2)}) collective-permute-start(bf16[160,2688]{1,0:T(8,128)(2,1)S(1)} %collective-permute-done.7.refs_0_), channel_id=1, source_target_pairs={{0,4},{1,3},{2,0},{3,7},{4,8},{5,1},{6,2},{7,11},{8,12},{9,5},{10,... | collective-permute-start | bytes 2580488 | tf_op jit(solution)/shard_map/ppermute | solution.py:464
  54.1 16.3 %collective-permute-start.12 = (bf16[160,2688]{1,0:T(8,128)(2,1)S(1)}, bf16[160,2688]{1,0:T(8,128)(2,1)S(1)}, u32[]{:S(2)}, u32[]{:S(2)}) collective-permute-start(bf16[160,2688]{1,0:T(8,128)(2,1)S(1)} %collective-permute-done.7.refs_0_), channel_id=1, source_target_pairs={{0,1},{1,0},{2,3},{3,2},{4,5},{5,4},{6,7},{7,6},{8,9},{9,8},{10,11... | collective-permute-start | bytes 2580488 | tf_op jit(solution)/shard_map/ppermute | solution.py:467
  61.2 9.2 %collective-permute-start.13 = (bf16[160,2688]{1,0:T(8,128)(2,1)S(1)}, bf16[160,2688]{1,0:T(8,128)(2,1)S(1)}, u32[]{:S(2)}, u32[]{:S(2)}) collective-permute-start(bf16[160,2688]{1,0:T(8,128)(2,1)S(1)} %collective-permute-done.10.refs_1_), channel_id=1, source_target_pairs={{0,1},{1,0},{2,3},{3,2},{4,5},{5,4},{6,7},{7,6},{8,9},{9,8},{10,11... | collective-permute-start | bytes 2580488 | tf_op jit(solution)/shard_map/ppermute | solution.py:467
  70.4 4.9 %collective-permute-start.14 = (bf16[160,2688]{1,0:T(8,128)(2,1)S(1)}, bf16[160,2688]{1,0:T(8,128)(2,1)S(1)}, u32[]{:S(2)}, u32[]{:S(2)}) collective-permute-start(bf16[160,2688]{1,0:T(8,128)(2,1)S(1)} %collective-permute-done.11.refs_0_), channel_id=1, source_target_pairs={{0,1},{1,0},{2,3},{3,2},{4,5},{5,4},{6,7},{7,6},{8,9},{9,8},{10,11... | collective-permute-start | bytes 2580488 | tf_op jit(solution)/shard_map/ppermute | solution.py:467
  84.3 5.0 %collective-permute-start.15 = (bf16[160,2560]{1,0:T(8,128)(2,1)S(1)}, bf16[160,2560]{1,0:T(8,128)(2,1)S(1)}, u32[]{:S(2)}, u32[]{:S(2)}) collective-permute-start(bf16[160,2560]{1,0:T(8,128)(2,1)S(1)} %get-tuple-element.126), channel_id=1, source_target_pairs={{0,1},{1,0},{2,3},{3,2},{4,5},{5,4},{6,7},{7,6},{8,9},{9,8},{10,11... | collective-permute-start | bytes 2457608 | tf_op jit(solution)/shard_map/ppermute | solution.py:467
  88.8 12.7 %collective-permute-start.16 = (bf16[160,2560]{1,0:T(8,128)(2,1)S(1)}, bf16[160,2560]{1,0:T(8,128)(2,1)S(1)}, u32[]{:S(2)}, u32[]{:S(2)}) collective-permute-start(bf16[160,2560]{1,0:T(8,128)(2,1)S(1)} %get-tuple-element.133), channel_id=1, source_target_pairs={{0,1},{1,0},{2,3},{3,2},{4,5},{5,4},{6,7},{7,6},{8,9},{9,8},{10,11... | collective-permute-start | bytes 2457608 | tf_op jit(solution)/shard_map/ppermute | solution.py:467
  88.8 6.8 %collective-permute-start.18 = (bf16[160,2560]{1,0:T(8,128)(2,1)S(1)}, bf16[160,2560]{1,0:T(8,128)(2,1)S(1)}, u32[]{:S(2)}, u32[]{:S(2)}) collective-permute-start(bf16[160,2560]{1,0:T(8,128)(2,1)S(1)} %get-tuple-element.136), channel_id=1, source_target_pairs={{0,1},{1,0},{2,3},{3,2},{4,5},{5,4},{6,7},{7,6},{8,9},{9,8},{10,11... | collective-permute-start | bytes 2457608 | tf_op jit(solution)/shard_map/ppermute | solution.py:467
  89.6 12.4 %collective-permute-start.17 = (bf16[160,2560]{1,0:T(8,128)(2,1)S(1)}, bf16[160,2560]{1,0:T(8,128)(2,1)S(1)}, u32[]{:S(2)}, u32[]{:S(2)}) collective-permute-start(bf16[160,2560]{1,0:T(8,128)(2,1)S(1)} %add_convert_fusion.8), channel_id=1, source_target_pairs={{0,4},{1,3},{2,0},{3,7},{4,8},{5,1},{6,2},{7,11},{8,12},{9,5},{10,... | collective-permute-start | bytes 2457608 | tf_op jit(solution)/shard_map/ppermute | solution.py:464
  99.7 19.2 %collective-permute-start.19 = (bf16[160,2560]{1,0:T(8,128)(2,1)S(1)}, bf16[160,2560]{1,0:T(8,128)(2,1)S(1)}, u32[]{:S(2)}, u32[]{:S(2)}) collective-permute-start(bf16[160,2560]{1,0:T(8,128)(2,1)S(1)} %get-tuple-element.144), channel_id=1, source_target_pairs={{0,1},{1,0},{2,3},{3,2},{4,5},{5,4},{6,7},{7,6},{8,9},{9,8},{10,11... | collective-permute-start | bytes 2457608 | tf_op jit(solution)/shard_map/ppermute | solution.py:467
  99.8 12.4 %collective-permute-start.22 = (bf16[160,2560]{1,0:T(8,128)(2,1)S(1)}, bf16[160,2560]{1,0:T(8,128)(2,1)S(1)}, u32[]{:S(2)}, u32[]{:S(2)}) collective-permute-start(bf16[160,2560]{1,0:T(8,128)(2,1)S(1)} %add_convert_fusion.6), channel_id=1, source_target_pairs={{0,4},{1,3},{2,0},{3,7},{4,8},{5,1},{6,2},{7,11},{8,12},{9,5},{10,... | collective-permute-start | bytes 2457608 | tf_op jit(solution)/shard_map/ppermute | solution.py:464
  101.4 10.8 %collective-permute-start.21 = (bf16[160,2560]{1,0:T(8,128)(2,1)S(1)}, bf16[160,2560]{1,0:T(8,128)(2,1)S(1)}, u32[]{:S(2)}, u32[]{:S(2)}) collective-permute-start(bf16[160,2560]{1,0:T(8,128)(2,1)S(1)} %get-tuple-element.147), channel_id=1, source_target_pairs={{0,1},{1,0},{2,3},{3,2},{4,5},{5,4},{6,7},{7,6},{8,9},{9,8},{10,11... | collective-permute-start | bytes 2457608 | tf_op jit(solution)/shard_map/ppermute | solution.py:467
  102.3 18.7 %collective-permute-start.20 = (bf16[160,2560]{1,0:T(8,128)(2,1)S(1)}, bf16[160,2560]{1,0:T(8,128)(2,1)S(1)}, u32[]{:S(2)}, u32[]{:S(2)}) collective-permute-start(bf16[160,2560]{1,0:T(8,128)(2,1)S(1)} %add_convert_fusion.7), channel_id=1, source_target_pairs={{0,4},{1,3},{2,0},{3,7},{4,8},{5,1},{6,2},{7,11},{8,12},{9,5},{10,... | collective-permute-start | bytes 2457608 | tf_op jit(solution)/shard_map/ppermute | solution.py:464
  117.3 17.7 %collective-permute-start.23 = (bf16[160,2560]{1,0:T(8,128)(2,1)S(1)}, bf16[160,2560]{1,0:T(8,128)(2,1)S(1)}, u32[]{:S(2)}, u32[]{:S(2)}) collective-permute-start(bf16[160,2560]{1,0:T(8,128)(2,1)S(1)} %get-tuple-element.156), channel_id=1, source_target_pairs={{0,1},{1,0},{2,3},{3,2},{4,5},{5,4},{6,7},{7,6},{8,9},{9,8},{10,11... | collective-permute-start | bytes 2457608 | tf_op jit(solution)/shard_map/ppermute | solution.py:467
  117.3 12.4 %collective-permute-start.26 = (bf16[160,2560]{1,0:T(8,128)(2,1)S(1)}, bf16[160,2560]{1,0:T(8,128)(2,1)S(1)}, u32[]{:S(2)}, u32[]{:S(2)}) collective-permute-start(bf16[160,2560]{1,0:T(8,128)(2,1)S(1)} %add_convert_fusion.4), channel_id=1, source_target_pairs={{0,4},{1,3},{2,0},{3,7},{4,8},{5,1},{6,2},{7,11},{8,12},{9,5},{10,... | collective-permute-start | bytes 2457608 | tf_op jit(solution)/shard_map/ppermute | solution.py:464
  119.0 10.8 %collective-permute-start.25 = (bf16[160,2560]{1,0:T(8,128)(2,1)S(1)}, bf16[160,2560]{1,0:T(8,128)(2,1)S(1)}, u32[]{:S(2)}, u32[]{:S(2)}) collective-permute-start(bf16[160,2560]{1,0:T(8,128)(2,1)S(1)} %get-tuple-element.159), channel_id=1, source_target_pairs={{0,1},{1,0},{2,3},{3,2},{4,5},{5,4},{6,7},{7,6},{8,9},{9,8},{10,11... | collective-permute-start | bytes 2457608 | tf_op jit(solution)/shard_map/ppermute | solution.py:467
  121.3 17.2 %collective-permute-start.24 = (bf16[160,2560]{1,0:T(8,128)(2,1)S(1)}, bf16[160,2560]{1,0:T(8,128)(2,1)S(1)}, u32[]{:S(2)}, u32[]{:S(2)}) collective-permute-start(bf16[160,2560]{1,0:T(8,128)(2,1)S(1)} %add_convert_fusion.5), channel_id=1, source_target_pairs={{0,4},{1,3},{2,0},{3,7},{4,8},{5,1},{6,2},{7,11},{8,12},{9,5},{10,... | collective-permute-start | bytes 2457608 | tf_op jit(solution)/shard_map/ppermute | solution.py:464
  130.1 17.2 %collective-permute-start.27 = (bf16[160,2560]{1,0:T(8,128)(2,1)S(1)}, bf16[160,2560]{1,0:T(8,128)(2,1)S(1)}, u32[]{:S(2)}, u32[]{:S(2)}) collective-permute-start(bf16[160,2560]{1,0:T(8,128)(2,1)S(1)} %add_convert_fusion.2), channel_id=1, source_target_pairs={{0,4},{1,3},{2,0},{3,7},{4,8},{5,1},{6,2},{7,11},{8,12},{9,5},{10,... | collective-permute-start | bytes 2457608 | tf_op jit(solution)/shard_map/ppermute | solution.py:464
  138.9 17.2 %collective-permute-start.29 = (bf16[160,2560]{1,0:T(8,128)(2,1)S(1)}, bf16[160,2560]{1,0:T(8,128)(2,1)S(1)}, u32[]{:S(2)}, u32[]{:S(2)}) collective-permute-start(bf16[160,2560]{1,0:T(8,128)(2,1)S(1)} %add_convert_fusion.3), channel_id=1, source_target_pairs={{0,4},{1,3},{2,0},{3,7},{4,8},{5,1},{6,2},{7,11},{8,12},{9,5},{10,... | collective-permute-start | bytes 2457608 | tf_op jit(solution)/shard_map/ppermute | solution.py:464
  147.6 8.5 %collective-permute-start.28 = (bf16[160,2560]{1,0:T(8,128)(2,1)S(1)}, bf16[160,2560]{1,0:T(8,128)(2,1)S(1)}, u32[]{:S(2)}, u32[]{:S(2)}) collective-permute-start(bf16[160,2560]{1,0:T(8,128)(2,1)S(1)} %add_convert_fusion.1), channel_id=1, source_target_pairs={{0,1},{1,0},{2,3},{3,2},{4,5},{5,4},{6,7},{7,6},{8,9},{9,8},{10,11... | collective-permute-start | bytes 2457608 | tf_op jit(solution)/shard_map/ppermute | solution.py:467
where the time goes:
time: 158 us; the launch traced here: 157 us
  Pallas kernels  84 us (53%)
  waiting for transfers between devices  38.7 us (24%)
  starting transfers between devices  30 us (19%)
  other arithmetic  3.62 us (2%)
    pallas_call x8, Pallas kernels, hidden_call(): pl.pallas_call(functools.partial(hidden_kernel, tuple(places), rows, chun...  46.5 us
    ppermute x14, waiting for transfers between devices, along(): return lax.ppermute(array, AXES, ring.step())  38.7 us
    pallas_call x9, Pallas kernels, down_call(): pl.pallas_call(functools.partial(down_kernel, groups, rows, text_rows, se...  36.2 us
    ppermute x14, starting transfers between devices, along(): return lax.ppermute(array, AXES, ring.step())  28.2 us
    convert_element_type x9, other arithmetic, add_up(): return total.astype(jnp.bfloat16)  3.62 us
  transfers between devices with their start and end apart: 30, of which 13 were waited for; matrix products, arithmetic and copies ran while one was open for 2% of the time, Pallas kernels for 47%

commit v1 on v0

--- a/solution.py
+++ b/solution.py
@@ -499,9 +499,12 @@
         next_trail = along(trail) if s + 1 < ring.half else None
         trail_across = across(trail)
         extra = down_weight if s == 1 else None
+        blocks, block_rows = [lead, trail], rows_of(4 * s, 4 * s + 1)
+        at_last = s + 1 == ring.half
+        if at_last:
+            blocks, block_rows = blocks + [lead_across], block_rows + rows_of(4 * s + 3)
         hidden, gate_up, *down = hidden_call(
-            [lead, trail], rows_of(4 * s, 4 * s + 1), gate_up, hidden, all_rows, extra,
-            unroll=s + 1 == ring.half,
+            blocks, block_rows, gate_up, hidden, all_rows, extra, unroll=at_last
         )
         if down:
             (down_here,) = down
@@ -509,7 +512,9 @@
             hidden, next_lead, lead_across, trail_across
         )
         trail = next_trail
-        swapped, swapped_rows = [lead_across, trail_across], rows_of(4 * s + 3, 4 * s + 2)
+        swapped, swapped_rows = [trail_across], rows_of(4 * s + 2)
+        if not at_last:
+            swapped, swapped_rows = swapped + [lead_across], swapped_rows + rows_of(4 * s + 3)
     hidden, gate_up = hidden_call(swapped, swapped_rows, gate_up, hidden, all_rows, unroll=True)
     far = [lead, across(lead)]
     (hidden,) = hidden_call(
@@ -545,10 +550,13 @@
     mine, hidden = for_own(hidden, ring.half - 1)
     trail, hidden = sent(hidden, mine[1], swapped[1])
     for s in range(ring.half - 1, 0, -1):
+        if s + 1 == ring.half:
+            lead, hidden = sent(hidden, mine[0], swapped[0], lead)
         next_swapped, hidden = for_other(hidden, s - 1)
         if s > 1:
             next_swapped = [across(array) for array in next_swapped]
-        lead, hidden = sent(hidden, mine[0], swapped[0], lead)
+        if s + 1 < ring.half:
+            lead, hidden = sent(hidden, mine[0], swapped[0], lead)
         mine, hidden = for_own(hidden, s - 1)
         swapped = next_swapped
         if s > 1:

time: 158 us -> 158 us (level)
  Pallas kernels: 84 us -> 86.3 us
    pallas_call x8, Pallas kernels: 46.5 us -> 48.8 us  [hidden_call(): pl.pallas_call(functools.partial(hidden_kernel, tuple(places), rows, chun...]
  transfers between devices with their start and end apart: 30 -> 30, of which waited for: 13 -> 11; matrix products, arithmetic and copies ran while one was open for 2% -> 2% of each run, Pallas kernels for 47% -> 48%
where the time goes in v1:
time: 158 us
  Pallas kernels  86.3 us (55%)
  waiting for transfers between devices  37.3 us (24%)
  starting transfers between devices  30.2 us (19%)
  other arithmetic  3.34 us (2%)
    pallas_call x8, Pallas kernels, hidden_call(): pl.pallas_call(functools.partial(hidden_kernel, tuple(places), rows, chun...  48.8 us
    ppermute x14, waiting for transfers between devices, along(): return lax.ppermute(array, AXES, ring.step())  37.3 us
    pallas_call x9, Pallas kernels, down_call(): pl.pallas_call(functools.partial(down_kernel, groups, rows, text_rows, se...  36.2 us
    ppermute x14, starting transfers between devices, along(): return lax.ppermute(array, AXES, ring.step())  28.3 us
    convert_element_type x9, other arithmetic, add_up(): return total.astype(jnp.bfloat16)  3.34 us
  transfers between devices with their start and end apart: 30, of which 11 were waited for; matrix products, arithmetic and copies ran while one was open for 2% of the time, Pallas kernels for 48%

profile of v1, /device:TPU:0, one launch (start us, length us, event | category | flops | bytes accessed | tf_op | source)
XLA Modules:
  0.0 158.1 jit_solution(12390484810077115540)
XLA Ops:
  1.8 2.6 %collective-permute-start.1 = (bf16[160,2688]{1,0:T(8,128)(2,1)S(1)}, bf16[160,2688]{1,0:T(8,128)(2,1)S(1)}, u32[]{:S(2)}, u32[]{:S(2)}) collective-permute-start(bf16[160,2688]{1,0:T(8,128)(2,1)S(1)} %shard_map.82.refs_0_), channel_id=1, source_target_pairs={{0,4},{1,3},{2,0},{3,7},{4,8},{5,1},{6,2},{7,11},{8,12},{9,5},{10,... | collective-permute-start | bytes 2580488 | tf_op jit(solution)/shard_map/ppermute | solution.py:464
  4.4 2.3 %collective-permute-start.2 = (bf16[160,2688]{1,0:T(8,128)(2,1)S(1)}, bf16[160,2688]{1,0:T(8,128)(2,1)S(1)}, u32[]{:S(2)}, u32[]{:S(2)}) collective-permute-start(bf16[160,2688]{1,0:T(8,128)(2,1)S(1)} %collective-permute-done.refs_1_), channel_id=1, source_target_pairs={{0,4},{1,3},{2,0},{3,7},{4,8},{5,1},{6,2},{7,11},{8,12},{9,5},{10,... | collective-permute-start | bytes 2580488 | tf_op jit(solution)/shard_map/ppermute | solution.py:464
  7.5 7.7 %shard_map.83 = (bf16[2560,1536]{1,0:T(8,128)(2,1)S(1)}, bf16[1,2,1408,2560]{3,2,1,0:T(8,128)(2,1)S(1)}) custom-call(bf16[160,2688]{1,0:T(8,128)(2,1)S(1)} %shard_map.82.refs_0_, bf16[160,2688]{1,0:T(8,128)(2,1)S(1)} %collective-permute-done.refs_1_, bf16[1,2,1408,2560]{3,2,1,0:T(8,128)(2,1)} %refs_2_.1), custom_call_target="tpu_custom_call" | custom-call | flops 4613734400 | bytes 16957440 | tf_op jit(solution)/shard_map/pallas_call | solution.py:350
  17.2 7.1 %collective-permute-done.2.refs_1_ = bf16[160,2688]{1,0:T(8,128)(2,1)S(1)} collective-permute-done((bf16[160,2688]{1,0:T(8,128)(2,1)S(1)}, bf16[160,2688]{1,0:T(8,128)(2,1)S(1)}, u32[]{:S(2)}, u32[]{:S(2)}) %collective-permute-start.2) | collective-permute-done | bytes 860192 | tf_op jit(solution)/shard_map/ppermute | solution.py:464
  24.3 2.1 %collective-permute-start.6 = (bf16[160,2688]{1,0:T(8,128)(2,1)S(1)}, bf16[160,2688]{1,0:T(8,128)(2,1)S(1)}, u32[]{:S(2)}, u32[]{:S(2)}) collective-permute-start(bf16[160,2688]{1,0:T(8,128)(2,1)S(1)} %collective-permute-done.2.refs_1_), channel_id=1, source_target_pairs={{0,4},{1,3},{2,0},{3,7},{4,8},{5,1},{6,2},{7,11},{8,12},{9,5},{10,... | collective-permute-start | bytes 2580488 | tf_op jit(solution)/shard_map/ppermute | solution.py:464
  26.4 6.0 %shard_map.84 = (bf16[2560,1536]{1,0:T(8,128)(2,1)S(1)}, bf16[1,2,1408,2560]{3,2,1,0:T(8,128)(2,1)S(1)}, bf16[1,1408,2560]{2,1,0:T(8,128)(2,1)S(1)}) custom-call(bf16[160,2688]{1,0:T(8,128)(2,1)S(1)} %collective-permute-done.1.refs_0_, bf16[160,2688]{1,0:T(8,128)(2,1)S(1)} %collective-permute-done.2.refs_1_, ...), custom_call_target="tpu_custom_call", output_to_operand_aliasing={{0}: (3, {}), {1}: (2, {})} | custom-call | flops 4613734400 | bytes 16957440 | tf_op jit(solution)/shard_map/pallas_call | solution.py:350
  33.6 2.1 %collective-permute-start.7 = (bf16[160,2688]{1,0:T(8,128)(2,1)S(1)}, bf16[160,2688]{1,0:T(8,128)(2,1)S(1)}, u32[]{:S(2)}, u32[]{:S(2)}) collective-permute-start(bf16[160,2688]{1,0:T(8,128)(2,1)S(1)} %collective-permute-done.3.refs_0_), channel_id=1, source_target_pairs={{0,4},{1,3},{2,0},{3,7},{4,8},{5,1},{6,2},{7,11},{8,12},{9,5},{10,... | collective-permute-start | bytes 2580488 | tf_op jit(solution)/shard_map/ppermute | solution.py:464
  35.7 6.0 %shard_map.85 = (bf16[2560,1536]{1,0:T(8,128)(2,1)S(1)}, bf16[1,2,1408,2560]{3,2,1,0:T(8,128)(2,1)S(1)}) custom-call(bf16[160,2688]{1,0:T(8,128)(2,1)S(1)} %collective-permute-done.5.refs_0_, bf16[160,2688]{1,0:T(8,128)(2,1)S(1)} %collective-permute-done.4.refs_1_, ...), custom_call_target="tpu_custom_call", output_to_operand_aliasing={{0}: (3, {}), {1}: (2, {})} | custom-call | flops 4613734400 | bytes 16957440 | tf_op jit(solution)/shard_map/pallas_call | solution.py:350
  42.8 2.1 %collective-permute-start.10 = (bf16[160,2688]{1,0:T(8,128)(2,1)S(1)}, bf16[160,2688]{1,0:T(8,128)(2,1)S(1)}, u32[]{:S(2)}, u32[]{:S(2)}) collective-permute-start(bf16[160,2688]{1,0:T(8,128)(2,1)S(1)} %collective-permute-done.6.refs_1_), channel_id=1, source_target_pairs={{0,4},{1,3},{2,0},{3,7},{4,8},{5,1},{6,2},{7,11},{8,12},{9,5},{10,... | collective-permute-start | bytes 2580488 | tf_op jit(solution)/shard_map/ppermute | solution.py:464
  44.9 6.0 %shard_map.86 = (bf16[2560,1536]{1,0:T(8,128)(2,1)S(1)}, bf16[1,2,1408,2560]{3,2,1,0:T(8,128)(2,1)S(1)}) custom-call(bf16[160,2688]{1,0:T(8,128)(2,1)S(1)} %collective-permute-done.3.refs_0_, bf16[160,2688]{1,0:T(8,128)(2,1)S(1)} %collective-permute-done.6.refs_1_, ...), custom_call_target="tpu_custom_call", output_to_operand_aliasing={{0}: (3, {}), {1}: (2, {})} | custom-call | flops 4613734400 | bytes 16957440 | tf_op jit(solution)/shard_map/pallas_call | solution.py:350
  52.0 2.2 %collective-permute-start.12 = (bf16[160,2688]{1,0:T(8,128)(2,1)S(1)}, bf16[160,2688]{1,0:T(8,128)(2,1)S(1)}, u32[]{:S(2)}, u32[]{:S(2)}) collective-permute-start(bf16[160,2688]{1,0:T(8,128)(2,1)S(1)} %collective-permute-done.7.refs_0_), channel_id=1, source_target_pairs={{0,4},{1,3},{2,0},{3,7},{4,8},{5,1},{6,2},{7,11},{8,12},{9,5},{10,... | collective-permute-start | bytes 2580488 | tf_op jit(solution)/shard_map/ppermute | solution.py:464
  54.2 6.2 %shard_map.87 = (bf16[2560,1536]{1,0:T(8,128)(2,1)S(1)}, bf16[1,2,1408,2560]{3,2,1,0:T(8,128)(2,1)S(1)}) custom-call(bf16[160,2688]{1,0:T(8,128)(2,1)S(1)} %collective-permute-done.9.refs_0_, bf16[160,2688]{1,0:T(8,128)(2,1)S(1)} %collective-permute-done.8.refs_1_, ...), custom_call_target="tpu_custom_call", output_to_operand_aliasing={{0}: (3, {}), {1}: (2, {})} | custom-call | flops 4613734400 | bytes 16957440 | tf_op jit(solution)/shard_map/pallas_call | solution.py:350
  61.2 7.2 %shard_map.88 = (bf16[2560,1536]{1,0:T(8,128)(2,1)S(1)}, bf16[1,2,1408,2560]{3,2,1,0:T(8,128)(2,1)S(1)}) custom-call(bf16[160,2688]{1,0:T(8,128)(2,1)S(1)} %collective-permute-done.7.refs_0_, bf16[160,2688]{1,0:T(8,128)(2,1)S(1)} %collective-permute-done.10.refs_1_, ...), custom_call_target="tpu_custom_call", output_to_operand_aliasing={{0}: (4, {}), {1}: (3, {})} | custom-call | flops 6920601600 | bytes 18227200 | tf_op jit(solution)/shard_map/pallas_call | solution.py:350
  70.4 4.8 %shard_map.89 = (bf16[2560,1536]{1,0:T(8,128)(2,1)S(1)}, bf16[1,2,1408,2560]{3,2,1,0:T(8,128)(2,1)S(1)}) custom-call(bf16[160,2688]{1,0:T(8,128)(2,1)S(1)} %collective-permute-done.13.refs_0_, bf16[1,2,1408,2560]{3,2,1,0:T(8,128)(2,1)S(1)} %get-tuple-element.117.refs_1_, ...), custom_call_target="tpu_custom_call", output_to_operand_aliasing={{0}: (2, {}), {1}: (1, {})} | custom-call | flops 2306867200 | bytes 15687680 | tf_op jit(solution)/shard_map/pallas_call | solution.py:350
  75.2 4.9 %shard_map.90.hidden_ref = bf16[2560,1536]{1,0:T(8,128)(2,1)S(1)} custom-call(bf16[160,2688]{1,0:T(8,128)(2,1)S(1)} %collective-permute-done.12.refs_0_, bf16[160,2688]{1,0:T(8,128)(2,1)S(1)} %collective-permute-done.14.refs_1_, bf16[1,2,1408,2560]{3,2,1,0:T(8,128)(2,1)S(1)} %get-tuple-element.119.refs_2_, ...), custom_call_target="tpu_custom_call", output_to_operand_aliasing={{}: (3, {})} | custom-call | flops 4613734400 | bytes 16957440 | tf_op jit(solution)/shard_map/pallas_call | solution.py:350
  80.1 4.1 %shard_map.91 = (bf16[160,2560]{1,0:T(8,128)(2,1)S(1)}, bf16[160,2560]{1,0:T(8,128)(2,1)S(1)}) custom-call(s32[81]{0:T(128)S(1)} %dynamic-slice_bitcast_fusion.places_ref, bf16[2560,1536]{1,0:T(8,128)(2,1)S(1)} %shard_map.90.hidden_ref, bf16[1,1408,2560]{2,1,0:T(8,128)(2,1)S(1)} %get-tuple-element.121.w_ref), custom_call_target="tpu_custom_call" | custom-call | flops 2306867200 | bytes 8847360 | tf_op jit(solution)/shard_map/pallas_call | solution.py:423
  84.8 3.9 %shard_map.92 = (bf16[160,2560]{1,0:T(8,128)(2,1)S(1)}, bf16[160,2560]{1,0:T(8,128)(2,1)S(1)}) custom-call(s32[81]{0:T(128)S(1)} %dynamic-slice_bitcast_fusion.places_ref, bf16[2560,1536]{1,0:T(8,128)(2,1)S(1)} %shard_map.90.hidden_ref, bf16[1,1408,2560]{2,1,0:T(8,128)(2,1)S(1)} %get-tuple-element.121.w_ref), custom_call_target="tpu_custom_call" | custom-call | flops 2306867200 | bytes 8847360 | tf_op jit(solution)/shard_map/pallas_call | solution.py:423
  89.5 2.2 %collective-permute-start.17 = (bf16[160,2560]{1,0:T(8,128)(2,1)S(1)}, bf16[160,2560]{1,0:T(8,128)(2,1)S(1)}, u32[]{:S(2)}, u32[]{:S(2)}) collective-permute-start(bf16[160,2560]{1,0:T(8,128)(2,1)S(1)} %add_convert_fusion.8), channel_id=1, source_target_pairs={{0,4},{1,3},{2,0},{3,7},{4,8},{5,1},{6,2},{7,11},{8,12},{9,5},{10,... | collective-permute-start | bytes 2457608 | tf_op jit(solution)/shard_map/ppermute | solution.py:464
  91.6 3.9 %shard_map.93 = (bf16[160,2560]{1,0:T(8,128)(2,1)S(1)}, bf16[160,2560]{1,0:T(8,128)(2,1)S(1)}) custom-call(s32[81]{0:T(128)S(1)} %dynamic-slice_bitcast_fusion.places_ref, bf16[2560,1536]{1,0:T(8,128)(2,1)S(1)} %shard_map.90.hidden_ref, bf16[1,1408,2560]{2,1,0:T(8,128)(2,1)S(1)} %get-tuple-element.121.w_ref), custom_call_target="tpu_custom_call" | custom-call | flops 2306867200 | bytes 8847360 | tf_op jit(solution)/shard_map/pallas_call | solution.py:423
  97.4 4.5 %collective-permute-done.17 = bf16[160,2560]{1,0:T(8,128)(2,1)S(1)} collective-permute-done((bf16[160,2560]{1,0:T(8,128)(2,1)S(1)}, bf16[160,2560]{1,0:T(8,128)(2,1)S(1)}, u32[]{:S(2)}, u32[]{:S(2)}) %collective-permute-start.17) | collective-permute-done | bytes 819232 | tf_op jit(solution)/shard_map/ppermute | solution.py:464
  102.2 3.9 %shard_map.94 = (bf16[160,2560]{1,0:T(8,128)(2,1)S(1)}, bf16[160,2560]{1,0:T(8,128)(2,1)S(1)}) custom-call(s32[81]{0:T(128)S(1)} %dynamic-slice_bitcast_fusion.places_ref, bf16[2560,1536]{1,0:T(8,128)(2,1)S(1)} %shard_map.90.hidden_ref, bf16[1,1408,2560]{2,1,0:T(8,128)(2,1)S(1)} %get-tuple-element.121.w_ref), custom_call_target="tpu_custom_call" | custom-call | flops 2306867200 | bytes 8847360 | tf_op jit(solution)/shard_map/pallas_call | solution.py:423
  106.2 2.2 %collective-permute-start.20 = (bf16[160,2560]{1,0:T(8,128)(2,1)S(1)}, bf16[160,2560]{1,0:T(8,128)(2,1)S(1)}, u32[]{:S(2)}, u32[]{:S(2)}) collective-permute-start(bf16[160,2560]{1,0:T(8,128)(2,1)S(1)} %add_convert_fusion.7), channel_id=1, source_target_pairs={{0,4},{1,3},{2,0},{3,7},{4,8},{5,1},{6,2},{7,11},{8,12},{9,5},{10,... | collective-permute-start | bytes 2457608 | tf_op jit(solution)/shard_map/ppermute | solution.py:464
  108.4 4.7 %shard_map.95 = (bf16[160,2560]{1,0:T(8,128)(2,1)S(1)}, bf16[160,2560]{1,0:T(8,128)(2,1)S(1)}) custom-call(s32[81]{0:T(128)S(1)} %dynamic-slice_bitcast_fusion.places_ref, bf16[2560,1536]{1,0:T(8,128)(2,1)S(1)} %shard_map.90.hidden_ref, bf16[1,1408,2560]{2,1,0:T(8,128)(2,1)S(1)} %get-tuple-element.121.w_ref), custom_call_target="tpu_custom_call" | custom-call | flops 2306867200 | bytes 8847360 | tf_op jit(solution)/shard_map/pallas_call | solution.py:423
  113.4 4.7 %shard_map.96 = (bf16[160,2560]{1,0:T(8,128)(2,1)S(1)}, bf16[160,2560]{1,0:T(8,128)(2,1)S(1)}) custom-call(s32[81]{0:T(128)S(1)} %dynamic-slice_bitcast_fusion.places_ref, bf16[2560,1536]{1,0:T(8,128)(2,1)S(1)} %shard_map.90.hidden_ref, bf16[1,1408,2560]{2,1,0:T(8,128)(2,1)S(1)} %get-tuple-element.121.w_ref), custom_call_target="tpu_custom_call" | custom-call | flops 2306867200 | bytes 8847360 | tf_op jit(solution)/shard_map/pallas_call | solution.py:423
  120.0 2.1 %collective-permute-start.24 = (bf16[160,2560]{1,0:T(8,128)(2,1)S(1)}, bf16[160,2560]{1,0:T(8,128)(2,1)S(1)}, u32[]{:S(2)}, u32[]{:S(2)}) collective-permute-start(bf16[160,2560]{1,0:T(8,128)(2,1)S(1)} %add_convert_fusion.5), channel_id=1, source_target_pairs={{0,4},{1,3},{2,0},{3,7},{4,8},{5,1},{6,2},{7,11},{8,12},{9,5},{10,... | collective-permute-start | bytes 2457608 | tf_op jit(solution)/shard_map/ppermute | solution.py:464
  122.2 4.7 %shard_map.97 = (bf16[160,2560]{1,0:T(8,128)(2,1)S(1)}, bf16[160,2560]{1,0:T(8,128)(2,1)S(1)}) custom-call(s32[81]{0:T(128)S(1)} %dynamic-slice_bitcast_fusion.places_ref, bf16[2560,1536]{1,0:T(8,128)(2,1)S(1)} %shard_map.90.hidden_ref, bf16[1,1408,2560]{2,1,0:T(8,128)(2,1)S(1)} %get-tuple-element.121.w_ref), custom_call_target="tpu_custom_call" | custom-call | flops 2306867200 | bytes 8847360 | tf_op jit(solution)/shard_map/pallas_call | solution.py:423
  126.8 3.7 %collective-permute-done.26 = bf16[160,2560]{1,0:T(8,128)(2,1)S(1)} collective-permute-done((bf16[160,2560]{1,0:T(8,128)(2,1)S(1)}, bf16[160,2560]{1,0:T(8,128)(2,1)S(1)}, u32[]{:S(2)}, u32[]{:S(2)}) %collective-permute-start.26) | collective-permute-done | bytes 819232 | tf_op jit(solution)/shard_map/ppermute | solution.py:464
  132.4 3.2 %shard_map.98 = bf16[160,2560]{1,0:T(8,128)(2,1)S(1)} custom-call(s32[81]{0:T(128)S(1)} %dynamic-slice_bitcast_fusion.places_ref, bf16[2560,1536]{1,0:T(8,128)(2,1)S(1)} %shard_map.90.hidden_ref, bf16[1,1408,2560]{2,1,0:T(8,128)(2,1)S(1)} %get-tuple-element.121.w_ref), custom_call_target="tpu_custom_call" | custom-call | flops 1153433600 | bytes 8028160 | tf_op jit(solution)/shard_map/pallas_call | solution.py:423
  135.6 3.7 %collective-permute-done.24 = bf16[160,2560]{1,0:T(8,128)(2,1)S(1)} collective-permute-done((bf16[160,2560]{1,0:T(8,128)(2,1)S(1)}, bf16[160,2560]{1,0:T(8,128)(2,1)S(1)}, u32[]{:S(2)}, u32[]{:S(2)}) %collective-permute-start.24) | collective-permute-done | bytes 819232 | tf_op jit(solution)/shard_map/ppermute | solution.py:464
  141.2 6.9 %collective-permute-done.27 = bf16[160,2560]{1,0:T(8,128)(2,1)S(1)} collective-permute-done((bf16[160,2560]{1,0:T(8,128)(2,1)S(1)}, bf16[160,2560]{1,0:T(8,128)(2,1)S(1)}, u32[]{:S(2)}, u32[]{:S(2)}) %collective-permute-start.27) | collective-permute-done | bytes 819232 | tf_op jit(solution)/shard_map/ppermute | solution.py:464
  148.4 3.2 %shard_map.99 = bf16[160,2560]{1,0:T(8,128)(2,1)S(1)} custom-call(s32[81]{0:T(128)S(1)} %dynamic-slice_bitcast_fusion.places_ref, bf16[2560,1536]{1,0:T(8,128)(2,1)S(1)} %shard_map.90.hidden_ref, bf16[1,1408,2560]{2,1,0:T(8,128)(2,1)S(1)} %get-tuple-element.121.w_ref), custom_call_target="tpu_custom_call" | custom-call | flops 1153433600 | bytes 8028160 | tf_op jit(solution)/shard_map/pallas_call | solution.py:423
  151.6 5.3 %collective-permute-done.29 = bf16[160,2560]{1,0:T(8,128)(2,1)S(1)} collective-permute-done((bf16[160,2560]{1,0:T(8,128)(2,1)S(1)}, bf16[160,2560]{1,0:T(8,128)(2,1)S(1)}, u32[]{:S(2)}, u32[]{:S(2)}) %collective-permute-start.29) | collective-permute-done | bytes 819232 | tf_op jit(solution)/shard_map/ppermute | solution.py:464
  (56 shorter events, 21.7 us)
Async XLA Ops:
  1.3 3.2 %collective-permute-start = (bf16[160,2688]{1,0:T(8,128)(2,1)S(1)}, bf16[160,2688]{1,0:T(8,128)(2,1)S(1)}, u32[]{:S(2)}, u32[]{:S(2)}) collective-permute-start(bf16[160,2688]{1,0:T(8,128)(2,1)S(1)} %shard_map.82.refs_0_), channel_id=1, source_target_pairs={{0,1},{1,0},{2,3},{3,2},{4,5},{5,4},{6,7},{7,6},{8,9},{9,8},{10,11... | collective-permute-start | bytes 2580488 | tf_op jit(solution)/shard_map/ppermute | solution.py:467
  1.8 13.4 %collective-permute-start.1 = (bf16[160,2688]{1,0:T(8,128)(2,1)S(1)}, bf16[160,2688]{1,0:T(8,128)(2,1)S(1)}, u32[]{:S(2)}, u32[]{:S(2)}) collective-permute-start(bf16[160,2688]{1,0:T(8,128)(2,1)S(1)} %shard_map.82.refs_0_), channel_id=1, source_target_pairs={{0,4},{1,3},{2,0},{3,7},{4,8},{5,1},{6,2},{7,11},{8,12},{9,5},{10,... | collective-permute-start | bytes 2580488 | tf_op jit(solution)/shard_map/ppermute | solution.py:464
  4.4 19.9 %collective-permute-start.2 = (bf16[160,2688]{1,0:T(8,128)(2,1)S(1)}, bf16[160,2688]{1,0:T(8,128)(2,1)S(1)}, u32[]{:S(2)}, u32[]{:S(2)}) collective-permute-start(bf16[160,2688]{1,0:T(8,128)(2,1)S(1)} %collective-permute-done.refs_1_), channel_id=1, source_target_pairs={{0,4},{1,3},{2,0},{3,7},{4,8},{5,1},{6,2},{7,11},{8,12},{9,5},{10,... | collective-permute-start | bytes 2580488 | tf_op jit(solution)/shard_map/ppermute | solution.py:464
  15.2 18.4 %collective-permute-start.3 = (bf16[160,2688]{1,0:T(8,128)(2,1)S(1)}, bf16[160,2688]{1,0:T(8,128)(2,1)S(1)}, u32[]{:S(2)}, u32[]{:S(2)}) collective-permute-start(bf16[160,2688]{1,0:T(8,128)(2,1)S(1)} %collective-permute-done.1.refs_0_), channel_id=1, source_target_pairs={{0,4},{1,3},{2,0},{3,7},{4,8},{5,1},{6,2},{7,11},{8,12},{9,5},{10,... | collective-permute-start | bytes 2580488 | tf_op jit(solution)/shard_map/ppermute | solution.py:464
  17.2 16.3 %collective-permute-start.4 = (bf16[160,2688]{1,0:T(8,128)(2,1)S(1)}, bf16[160,2688]{1,0:T(8,128)(2,1)S(1)}, u32[]{:S(2)}, u32[]{:S(2)}) collective-permute-start(bf16[160,2688]{1,0:T(8,128)(2,1)S(1)} %collective-permute-done.1.refs_0_), channel_id=1, source_target_pairs={{0,1},{1,0},{2,3},{3,2},{4,5},{5,4},{6,7},{7,6},{8,9},{9,8},{10,11... | collective-permute-start | bytes 2580488 | tf_op jit(solution)/shard_map/ppermute | solution.py:467
  24.3 9.2 %collective-permute-start.5 = (bf16[160,2688]{1,0:T(8,128)(2,1)S(1)}, bf16[160,2688]{1,0:T(8,128)(2,1)S(1)}, u32[]{:S(2)}, u32[]{:S(2)}) collective-permute-start(bf16[160,2688]{1,0:T(8,128)(2,1)S(1)} %collective-permute-done.2.refs_1_), channel_id=1, source_target_pairs={{0,1},{1,0},{2,3},{3,2},{4,5},{5,4},{6,7},{7,6},{8,9},{9,8},{10,11... | collective-permute-start | bytes 2580488 | tf_op jit(solution)/shard_map/ppermute | solution.py:467
  24.3 18.4 %collective-permute-start.6 = (bf16[160,2688]{1,0:T(8,128)(2,1)S(1)}, bf16[160,2688]{1,0:T(8,128)(2,1)S(1)}, u32[]{:S(2)}, u32[]{:S(2)}) collective-permute-start(bf16[160,2688]{1,0:T(8,128)(2,1)S(1)} %collective-permute-done.2.refs_1_), channel_id=1, source_target_pairs={{0,4},{1,3},{2,0},{3,7},{4,8},{5,1},{6,2},{7,11},{8,12},{9,5},{10,... | collective-permute-start | bytes 2580488 | tf_op jit(solution)/shard_map/ppermute | solution.py:464
  33.6 18.4 %collective-permute-start.7 = (bf16[160,2688]{1,0:T(8,128)(2,1)S(1)}, bf16[160,2688]{1,0:T(8,128)(2,1)S(1)}, u32[]{:S(2)}, u32[]{:S(2)}) collective-permute-start(bf16[160,2688]{1,0:T(8,128)(2,1)S(1)} %collective-permute-done.3.refs_0_), channel_id=1, source_target_pairs={{0,4},{1,3},{2,0},{3,7},{4,8},{5,1},{6,2},{7,11},{8,12},{9,5},{10,... | collective-permute-start | bytes 2580488 | tf_op jit(solution)/shard_map/ppermute | solution.py:464
  35.7 16.3 %collective-permute-start.8 = (bf16[160,2688]{1,0:T(8,128)(2,1)S(1)}, bf16[160,2688]{1,0:T(8,128)(2,1)S(1)}, u32[]{:S(2)}, u32[]{:S(2)}) collective-permute-start(bf16[160,2688]{1,0:T(8,128)(2,1)S(1)} %collective-permute-done.3.refs_0_), channel_id=1, source_target_pairs={{0,1},{1,0},{2,3},{3,2},{4,5},{5,4},{6,7},{7,6},{8,9},{9,8},{10,11... | collective-permute-start | bytes 2580488 | tf_op jit(solution)/shard_map/ppermute | solution.py:467
  42.8 9.2 %collective-permute-start.9 = (bf16[160,2688]{1,0:T(8,128)(2,1)S(1)}, bf16[160,2688]{1,0:T(8,128)(2,1)S(1)}, u32[]{:S(2)}, u32[]{:S(2)}) collective-permute-start(bf16[160,2688]{1,0:T(8,128)(2,1)S(1)} %collective-permute-done.6.refs_1_), channel_id=1, source_target_pairs={{0,1},{1,0},{2,3},{3,2},{4,5},{5,4},{6,7},{7,6},{8,9},{9,8},{10,11... | collective-permute-start | bytes 2580488 | tf_op jit(solution)/shard_map/ppermute | solution.py:467
  42.8 18.4 %collective-permute-start.10 = (bf16[160,2688]{1,0:T(8,128)(2,1)S(1)}, bf16[160,2688]{1,0:T(8,128)(2,1)S(1)}, u32[]{:S(2)}, u32[]{:S(2)}) collective-permute-start(bf16[160,2688]{1,0:T(8,128)(2,1)S(1)} %collective-permute-done.6.refs_1_), channel_id=1, source_target_pairs={{0,4},{1,3},{2,0},{3,7},{4,8},{5,1},{6,2},{7,11},{8,12},{9,5},{10,... | collective-permute-start | bytes 2580488 | tf_op jit(solution)/shard_map/ppermute | solution.py:464
  52.0 9.2 %collective-permute-start.11 = (bf16[160,2688]{1,0:T(8,128)(2,1)S(1)}, bf16[160,2688]{1,0:T(8,128)(2,1)S(1)}, u32[]{:S(2)}, u32[]{:S(2)}) collective-permute-start(bf16[160,2688]{1,0:T(8,128)(2,1)S(1)} %collective-permute-done.7.refs_0_), channel_id=1, source_target_pairs={{0,1},{1,0},{2,3},{3,2},{4,5},{5,4},{6,7},{7,6},{8,9},{9,8},{10,11... | collective-permute-start | bytes 2580488 | tf_op jit(solution)/shard_map/ppermute | solution.py:467
  52.0 18.4 %collective-permute-start.12 = (bf16[160,2688]{1,0:T(8,128)(2,1)S(1)}, bf16[160,2688]{1,0:T(8,128)(2,1)S(1)}, u32[]{:S(2)}, u32[]{:S(2)}) collective-permute-start(bf16[160,2688]{1,0:T(8,128)(2,1)S(1)} %collective-permute-done.7.refs_0_), channel_id=1, source_target_pairs={{0,4},{1,3},{2,0},{3,7},{4,8},{5,1},{6,2},{7,11},{8,12},{9,5},{10,... | collective-permute-start | bytes 2580488 | tf_op jit(solution)/shard_map/ppermute | solution.py:464
  61.2 9.2 %collective-permute-start.13 = (bf16[160,2688]{1,0:T(8,128)(2,1)S(1)}, bf16[160,2688]{1,0:T(8,128)(2,1)S(1)}, u32[]{:S(2)}, u32[]{:S(2)}) collective-permute-start(bf16[160,2688]{1,0:T(8,128)(2,1)S(1)} %collective-permute-done.10.refs_1_), channel_id=1, source_target_pairs={{0,1},{1,0},{2,3},{3,2},{4,5},{5,4},{6,7},{7,6},{8,9},{9,8},{10,11... | collective-permute-start | bytes 2580488 | tf_op jit(solution)/shard_map/ppermute | solution.py:467
  70.4 4.8 %collective-permute-start.14 = (bf16[160,2688]{1,0:T(8,128)(2,1)S(1)}, bf16[160,2688]{1,0:T(8,128)(2,1)S(1)}, u32[]{:S(2)}, u32[]{:S(2)}) collective-permute-start(bf16[160,2688]{1,0:T(8,128)(2,1)S(1)} %collective-permute-done.12.refs_0_), channel_id=1, source_target_pairs={{0,1},{1,0},{2,3},{3,2},{4,5},{5,4},{6,7},{7,6},{8,9},{9,8},{10,11... | collective-permute-start | bytes 2580488 | tf_op jit(solution)/shard_map/ppermute | solution.py:467
  84.2 5.0 %collective-permute-start.15 = (bf16[160,2560]{1,0:T(8,128)(2,1)S(1)}, bf16[160,2560]{1,0:T(8,128)(2,1)S(1)}, u32[]{:S(2)}, u32[]{:S(2)}) collective-permute-start(bf16[160,2560]{1,0:T(8,128)(2,1)S(1)} %get-tuple-element.124), channel_id=1, source_target_pairs={{0,1},{1,0},{2,3},{3,2},{4,5},{5,4},{6,7},{7,6},{8,9},{9,8},{10,11... | collective-permute-start | bytes 2457608 | tf_op jit(solution)/shard_map/ppermute | solution.py:467
  88.7 8.7 %collective-permute-start.16 = (bf16[160,2560]{1,0:T(8,128)(2,1)S(1)}, bf16[160,2560]{1,0:T(8,128)(2,1)S(1)}, u32[]{:S(2)}, u32[]{:S(2)}) collective-permute-start(bf16[160,2560]{1,0:T(8,128)(2,1)S(1)} %get-tuple-element.131), channel_id=1, source_target_pairs={{0,1},{1,0},{2,3},{3,2},{4,5},{5,4},{6,7},{7,6},{8,9},{9,8},{10,11... | collective-permute-start | bytes 2457608 | tf_op jit(solution)/shard_map/ppermute | solution.py:467
  88.8 6.8 %collective-permute-start.18 = (bf16[160,2560]{1,0:T(8,128)(2,1)S(1)}, bf16[160,2560]{1,0:T(8,128)(2,1)S(1)}, u32[]{:S(2)}, u32[]{:S(2)}) collective-permute-start(bf16[160,2560]{1,0:T(8,128)(2,1)S(1)} %get-tuple-element.134), channel_id=1, source_target_pairs={{0,1},{1,0},{2,3},{3,2},{4,5},{5,4},{6,7},{7,6},{8,9},{9,8},{10,11... | collective-permute-start | bytes 2457608 | tf_op jit(solution)/shard_map/ppermute | solution.py:467
  89.5 12.4 %collective-permute-start.17 = (bf16[160,2560]{1,0:T(8,128)(2,1)S(1)}, bf16[160,2560]{1,0:T(8,128)(2,1)S(1)}, u32[]{:S(2)}, u32[]{:S(2)}) collective-permute-start(bf16[160,2560]{1,0:T(8,128)(2,1)S(1)} %add_convert_fusion.8), channel_id=1, source_target_pairs={{0,4},{1,3},{2,0},{3,7},{4,8},{5,1},{6,2},{7,11},{8,12},{9,5},{10,... | collective-permute-start | bytes 2457608 | tf_op jit(solution)/shard_map/ppermute | solution.py:464
  95.7 17.4 %collective-permute-start.22 = (bf16[160,2560]{1,0:T(8,128)(2,1)S(1)}, bf16[160,2560]{1,0:T(8,128)(2,1)S(1)}, u32[]{:S(2)}, u32[]{:S(2)}) collective-permute-start(bf16[160,2560]{1,0:T(8,128)(2,1)S(1)} %add_convert_fusion.6), channel_id=1, source_target_pairs={{0,4},{1,3},{2,0},{3,7},{4,8},{5,1},{6,2},{7,11},{8,12},{9,5},{10,... | collective-permute-start | bytes 2457608 | tf_op jit(solution)/shard_map/ppermute | solution.py:464
  106.1 7.0 %collective-permute-start.21 = (bf16[160,2560]{1,0:T(8,128)(2,1)S(1)}, bf16[160,2560]{1,0:T(8,128)(2,1)S(1)}, u32[]{:S(2)}, u32[]{:S(2)}) collective-permute-start(bf16[160,2560]{1,0:T(8,128)(2,1)S(1)} %get-tuple-element.145), channel_id=1, source_target_pairs={{0,1},{1,0},{2,3},{3,2},{4,5},{5,4},{6,7},{7,6},{8,9},{9,8},{10,11... | collective-permute-start | bytes 2457608 | tf_op jit(solution)/shard_map/ppermute | solution.py:467
  106.2 13.5 %collective-permute-start.20 = (bf16[160,2560]{1,0:T(8,128)(2,1)S(1)}, bf16[160,2560]{1,0:T(8,128)(2,1)S(1)}, u32[]{:S(2)}, u32[]{:S(2)}) collective-permute-start(bf16[160,2560]{1,0:T(8,128)(2,1)S(1)} %add_convert_fusion.7), channel_id=1, source_target_pairs={{0,4},{1,3},{2,0},{3,7},{4,8},{5,1},{6,2},{7,11},{8,12},{9,5},{10,... | collective-permute-start | bytes 2457608 | tf_op jit(solution)/shard_map/ppermute | solution.py:464
  108.4 11.3 %collective-permute-start.19 = (bf16[160,2560]{1,0:T(8,128)(2,1)S(1)}, bf16[160,2560]{1,0:T(8,128)(2,1)S(1)}, u32[]{:S(2)}, u32[]{:S(2)}) collective-permute-start(bf16[160,2560]{1,0:T(8,128)(2,1)S(1)} %get-tuple-element.142), channel_id=1, source_target_pairs={{0,1},{1,0},{2,3},{3,2},{4,5},{5,4},{6,7},{7,6},{8,9},{9,8},{10,11... | collective-permute-start | bytes 2457608 | tf_op jit(solution)/shard_map/ppermute | solution.py:467
  118.1 12.4 %collective-permute-start.26 = (bf16[160,2560]{1,0:T(8,128)(2,1)S(1)}, bf16[160,2560]{1,0:T(8,128)(2,1)S(1)}, u32[]{:S(2)}, u32[]{:S(2)}) collective-permute-start(bf16[160,2560]{1,0:T(8,128)(2,1)S(1)} %add_convert_fusion.4), channel_id=1, source_target_pairs={{0,4},{1,3},{2,0},{3,7},{4,8},{5,1},{6,2},{7,11},{8,12},{9,5},{10,... | collective-permute-start | bytes 2457608 | tf_op jit(solution)/shard_map/ppermute | solution.py:464
  119.7 10.8 %collective-permute-start.25 = (bf16[160,2560]{1,0:T(8,128)(2,1)S(1)}, bf16[160,2560]{1,0:T(8,128)(2,1)S(1)}, u32[]{:S(2)}, u32[]{:S(2)}) collective-permute-start(bf16[160,2560]{1,0:T(8,128)(2,1)S(1)} %get-tuple-element.157), channel_id=1, source_target_pairs={{0,1},{1,0},{2,3},{3,2},{4,5},{5,4},{6,7},{7,6},{8,9},{9,8},{10,11... | collective-permute-start | bytes 2457608 | tf_op jit(solution)/shard_map/ppermute | solution.py:467
  120.0 19.3 %collective-permute-start.24 = (bf16[160,2560]{1,0:T(8,128)(2,1)S(1)}, bf16[160,2560]{1,0:T(8,128)(2,1)S(1)}, u32[]{:S(2)}, u32[]{:S(2)}) collective-permute-start(bf16[160,2560]{1,0:T(8,128)(2,1)S(1)} %add_convert_fusion.5), channel_id=1, source_target_pairs={{0,4},{1,3},{2,0},{3,7},{4,8},{5,1},{6,2},{7,11},{8,12},{9,5},{10,... | collective-permute-start | bytes 2457608 | tf_op jit(solution)/shard_map/ppermute | solution.py:464
  122.2 17.2 %collective-permute-start.23 = (bf16[160,2560]{1,0:T(8,128)(2,1)S(1)}, bf16[160,2560]{1,0:T(8,128)(2,1)S(1)}, u32[]{:S(2)}, u32[]{:S(2)}) collective-permute-start(bf16[160,2560]{1,0:T(8,128)(2,1)S(1)} %get-tuple-element.154), channel_id=1, source_target_pairs={{0,1},{1,0},{2,3},{3,2},{4,5},{5,4},{6,7},{7,6},{8,9},{9,8},{10,11... | collective-permute-start | bytes 2457608 | tf_op jit(solution)/shard_map/ppermute | solution.py:467
  130.8 17.3 %collective-permute-start.27 = (bf16[160,2560]{1,0:T(8,128)(2,1)S(1)}, bf16[160,2560]{1,0:T(8,128)(2,1)S(1)}, u32[]{:S(2)}, u32[]{:S(2)}) collective-permute-start(bf16[160,2560]{1,0:T(8,128)(2,1)S(1)} %add_convert_fusion.2), channel_id=1, source_target_pairs={{0,4},{1,3},{2,0},{3,7},{4,8},{5,1},{6,2},{7,11},{8,12},{9,5},{10,... | collective-permute-start | bytes 2457608 | tf_op jit(solution)/shard_map/ppermute | solution.py:464
  139.7 17.2 %collective-permute-start.29 = (bf16[160,2560]{1,0:T(8,128)(2,1)S(1)}, bf16[160,2560]{1,0:T(8,128)(2,1)S(1)}, u32[]{:S(2)}, u32[]{:S(2)}) collective-permute-start(bf16[160,2560]{1,0:T(8,128)(2,1)S(1)} %add_convert_fusion.3), channel_id=1, source_target_pairs={{0,4},{1,3},{2,0},{3,7},{4,8},{5,1},{6,2},{7,11},{8,12},{9,5},{10,... | collective-permute-start | bytes 2457608 | tf_op jit(solution)/shard_map/ppermute | solution.py:464
  148.3 8.6 %collective-permute-start.28 = (bf16[160,2560]{1,0:T(8,128)(2,1)S(1)}, bf16[160,2560]{1,0:T(8,128)(2,1)S(1)}, u32[]{:S(2)}, u32[]{:S(2)}) collective-permute-start(bf16[160,2560]{1,0:T(8,128)(2,1)S(1)} %add_convert_fusion.1), channel_id=1, source_target_pairs={{0,1},{1,0},{2,3},{3,2},{4,5},{5,4},{6,7},{7,6},{8,9},{9,8},{10,11... | collective-permute-start | bytes 2457608 | tf_op jit(solution)/shard_map/ppermute | solution.py:467
